TPU v7x, 32 devices: a whole 2x2x4 slice. The times are simulated.
32 devices in a mesh: node: 8 (over z, y), feat: 4 (over x, core).
Axes of the slice: x: 2, y: 2, z: 4, core: 2. Of those that a mesh axis runs over, the one named last changes fastest.
Arguments:
- feature_table: bfloat16 [16384, 768], P('node', 'feat'), may hold values from -6 to 6
- weights: bfloat16 [2, 768, 1024], P(None, 'feat'), may hold values from -0.21875 to 0.21875
- request_rows: int32 [8, 8, 6], P('node'), may hold values from 0 to 2047
- request_counts: int32 [8, 8], P('node'), may hold values from 1 to 6, as said below
- neighbors: int32 [2048, 5], P('node'), may hold values from 0 to 47, as said below
- nbr_counts: int32 [2048], P('node'), may hold values from 1 to 5, as said below
- self_rows: int32 [2048], P('node'), may hold values from 0 to 47, as said below
- grad_hidden: bfloat16 [2048, 1024], P('node'), may hold values from -0.046875 to 0.046875
Outputs:
- hidden: bfloat16 [2048, 1024], P(('node', 'feat'))
- weight_grad: float32 [2, 768, 1024], P(None, 'feat')
Inputs may be any that keep to these rules, and one draw needn't show every extreme that they name: `request_counts`: every node index asks each owner for at most 6 rows; in every draw some owner gets exactly 6 from every node index. `neighbors`: each entry is o * 6 + s for an owner o and a slot s below request_counts of the target's node index and o, entries beyond nbr_counts too. `self_rows`: likewise a live slot o * 6 + s of the target's node index. `nbr_counts`: some target of every node index has 5.
All inputs are finite; a program needn't handle non-finite values.
Results may differ from a plain program's by a relative error of at most 0.0033.
Values may be sent and summed in bfloat16 or wider, within the bound.
A program may use at most 64 MiB of HBM per device.

v0:
```python
import jax
import jax.numpy as jnp
from jax import lax
from jax.sharding import PartitionSpec as P


def smooth_gate(values):
    return (
        0.5
        * values
        * (1.0 + jnp.tanh(0.7978845608 * (values + 0.044715 * values * values * values)))
    )


def activate(preact, upstream):
    output, pullback = jax.vjp(smooth_gate, preact)
    slope = pullback(upstream.astype(jnp.float32))[0]
    return (output.astype(jnp.bfloat16), slope.astype(jnp.bfloat16))


def aggregate(frontier, local_nbrs, local_counts):
    picked = frontier[local_nbrs]
    within = jnp.arange(local_nbrs.shape[1], dtype=jnp.int32)[None, :] < local_counts[:, None]
    summed = jnp.sum(
        jnp.where(within[:, :, None], picked, jnp.zeros_like(picked)), axis=1, dtype=jnp.float32
    )
    return (summed / local_counts[:, None].astype(jnp.float32)).astype(jnp.bfloat16)


def project(own_rows, averaged, weights):
    first = jnp.dot(own_rows, weights[0], preferred_element_type=jnp.float32)
    return first + jnp.dot(averaged, weights[1], preferred_element_type=jnp.float32)


def contract(left_side, right_side):
    return lax.dot_general(
        left_side, right_side, (((0,), (0,)), ((), ())), preferred_element_type=jnp.float32
    )


def per_device(
    feature_table,
    weights,
    request_rows,
    request_counts,
    neighbors,
    nbr_counts,
    self_rows,
    grad_hidden,
):
    slot_count = request_rows.shape[2]
    looked = feature_table[
        lax.all_to_all(request_rows[0], "node", split_axis=0, concat_axis=0, tiled=True)
    ]
    fetched = lax.all_to_all(looked, "node", split_axis=0, concat_axis=0, tiled=True)
    filled = jnp.arange(slot_count, dtype=jnp.int32)[None, :] < request_counts[0][:, None]
    frontier = jnp.where(filled[:, :, None], fetched, jnp.zeros_like(fetched)).reshape(
        -1, fetched.shape[2]
    )
    own_rows = frontier[self_rows]
    averaged = aggregate(frontier, neighbors, nbr_counts)
    groups = lax.axis_size("feat")
    portion = own_rows.shape[0] // groups
    preact = lax.psum(project(own_rows, averaged, weights), "feat")
    output_all, slope = activate(preact, grad_hidden)
    hidden = lax.dynamic_slice_in_dim(output_all, lax.axis_index("feat") * portion, portion, 0)
    grad_terms = jnp.stack([contract(own_rows, slope), contract(averaged, slope)])
    weight_grad = lax.psum(grad_terms, "node")
    return (hidden, weight_grad)


def solution(mesh):
    placed = (
        P("node", "feat"),
        P(None, "feat", None),
        P("node", None, None),
        P("node", None),
        P("node", None),
        P("node"),
        P("node"),
        P("node", None),
    )
    return jax.shard_map(
        per_device,
        mesh=mesh,
        in_specs=placed,
        out_specs=(P(("node", "feat"), None), P(None, "feat", None)),
        check_vma=False,
    )
```

profile of v0, /device:TPU:0, one launch (start us, length us, event | category | flops | bytes accessed | tf_op | source)
XLA Modules:
  0.0 181.4 jit_solution(16425660642210178685)
XLA Ops:
  7.2 0.0 copy-start.2
  7.2 1.4 copy.20
  8.5 7.3 %all-to-all-start = ((s32[8,1,6]{2,1,0:T(1,128)}), s32[8,1,6]{2,1,0:T(1,128)S(1)}, u32[]{:S(2)}, u32[]{:S(2)}) async-start(s32[8,1,6]{2,1,0:T(1,128)} %copy.20), calls=%async_computation | async-start | bytes 8192 | tf_op jit(solution)/shard_map/all_to_all | solution.py:53
  15.8 0.7 iota_compare_fusion.1
  16.5 0.7 compare_select_fusion.2
  17.2 0.7 compare_select_fusion
  17.9 0.1 copy.24
  18.1 0.2 reshape.104
  18.3 0.8 iota_compare_fusion
  19.1 1.4 copy.23
  20.5 1.7 all-to-all-done
  22.2 0.1 copy.21
  22.3 0.1 copy.22
  22.4 0.1 reshape.88
  22.5 0.7 gather_fusion
  23.1 0.6 reshape.87
  23.8 4.3 %all-to-all-start.1 = ((bf16[8,6,192]{2,1,0:T(8,128)(2,1)}), bf16[8,6,192]{2,1,0:T(8,128)(2,1)S(1)}, u32[]{:S(2)}, u32[]{:S(2)}) async-start(bf16[8,6,192]{2,1,0:T(8,128)(2,1)} %reshape.87), calls=%async_computation.1 | async-start | bytes 65536 | tf_op jit(solution)/shard_map/all_to_all | solution.py:55
  28.1 0.0 all-reduce.3.cloned.1.call-start
  28.2 0.0 copy-done.2
  28.2 6.6 %all-to-all-done.1 = bf16[8,6,192]{2,1,0:T(8,128)(2,1)S(1)} async-done(((bf16[8,6,192]{2,1,0:T(8,128)(2,1)}), bf16[8,6,192]{2,1,0:T(8,128)(2,1)S(1)}, u32[]{:S(2)}, u32[]{:S(2)}) %all-to-all-start.1) | async-done | bytes 18464 | tf_op jit(solution)/shard_map/all_to_all | solution.py:55
  34.8 0.1 broadcast_select_fusion
  34.9 1.2 gather_fusion.1
  36.0 4.1 %gather_fusion.2 = bf16[1280,192]{1,0:T(8,128)(2,1)S(1)} fusion(bf16[48,192]{1,0:T(8,128)(2,1)S(1)} %reshape.85, s32[2048]{0:T(1024)S(1)} %pad_clamp_fusion), kind=kCustom, calls=%fused_computation.2 | custom fusion | bytes 988160 | tf_op jit(solution)/shard_map/gather | solution.py:22
  40.1 0.0 copy-start
  40.1 0.3 reshape.103
  40.4 0.8 copy-done
  41.2 0.3 fusion.11
  41.5 1.5 convert_reduce_fusion
  43.0 0.0 copy-start.1
  43.0 1.3 convolution_add_fusion
  44.4 0.0 all-reduce.3.cloned.1.call-update
  44.4 0.0 all-reduce.5.cloned.1.call-start
  44.4 33.6 %all-reduce.3.cloned.1.call-done = f32[256,1024]{1,0:T(8,128)} async-done(((f32[256,1024]{1,0:T(8,128)}), f32[256,1024]{1,0:T(8,128)}) %all-reduce.3.cloned.1.call-update) | async-done | bytes 1048592 | tf_op jit(solution)/shard_map/psum | solution.py:64
  78.0 0.0 copy-done.1
  78.0 2.1 %fusion.4 = (bf16[256,1024]{1,0:T(8,128)(2,1)S(1)}, f32[256,1024]{1,0:T(8,128)S(1)}, f32[256,1024]{1,0:T(8,128)S(1)}) fusion(bf16[256,1024]{1,0:T(8,128)(2,1)S(1)} %copy-done.1, f32[256,1024]{1,0:T(8,128)} %all-reduce.3.cloned.1.call-done), kind=kLoop, calls=%fused_computation.18 | loop fusion | flops 6553600 | bytes 4194304 | tf_op jit(solution)/shard_map/convert_element_type | solution.py:18
  80.2 0.4 convolution_bitcast_fusion
  80.6 0.3 convolution_bitcast_fusion.1
  80.9 1.2 pad_maximum_fusion
  82.1 0.0 all-reduce.5.cloned.1.call-update
  82.1 0.7 fusion.15
  82.8 89.0 %all-reduce.5.cloned.1.call-done = f32[2,192,1024]{2,1,0:T(8,128)} async-done(((f32[2,192,1024]{2,1,0:T(8,128)}), f32[2,192,1024]{2,1,0:T(8,128)}) %all-reduce.5.cloned.1.call-update) | async-done | bytes 1572880 | tf_op jit(solution)/shard_map/psum | solution.py:68
  171.8 2.7 %copy.27 = f32[2,192,1024]{2,1,0:T(8,128)} copy(f32[2,192,1024]{2,1,0:T(8,128)} %all-reduce.5.cloned.1.call-done) | data formatting | bytes 3145728
  (6 shorter events, 0.1 us)
Async XLA Ops:
  7.2 21.0 %copy-start.2 = (s32[256]{0:T(256)S(1)}, s32[256]{0:T(256)}, u32[]{:S(2)}) copy-start(s32[256]{0:T(256)} %param.13) | copy-start | bytes 3076
  8.5 13.7 %all-to-all-start = ((s32[8,1,6]{2,1,0:T(1,128)}), s32[8,1,6]{2,1,0:T(1,128)S(1)}, u32[]{:S(2)}, u32[]{:S(2)}) async-start(s32[8,1,6]{2,1,0:T(1,128)} %copy.20), calls=%async_computation | async-start | bytes 8192 | tf_op jit(solution)/shard_map/all_to_all | solution.py:53
  23.8 11.0 %all-to-all-start.1 = ((bf16[8,6,192]{2,1,0:T(8,128)(2,1)}), bf16[8,6,192]{2,1,0:T(8,128)(2,1)S(1)}, u32[]{:S(2)}, u32[]{:S(2)}) async-start(bf16[8,6,192]{2,1,0:T(8,128)(2,1)} %reshape.87), calls=%async_computation.1 | async-start | bytes 65536 | tf_op jit(solution)/shard_map/all_to_all | solution.py:55
  28.1 50.0 %all-reduce.3.cloned.1.call-start = ((), (), s32[]{:S(2)}) async-start(), calls=%async_computation.2 | async-start | bytes 2097152 | tf_op jit(solution)/shard_map/psum | solution.py:64
  40.1 1.1 copy-start
  43.0 35.0 %copy-start.1 = (bf16[256,1024]{1,0:T(8,128)(2,1)S(1)}, bf16[256,1024]{1,0:T(8,128)(2,1)}, u32[]{:S(2)}) copy-start(bf16[256,1024]{1,0:T(8,128)(2,1)} %param.15) | copy-start | bytes 1572868
  44.4 127.4 %all-reduce.5.cloned.1.call-start = ((), (), s32[]{:S(2)}) async-start(), calls=%async_computation.3 | async-start | bytes 3145728 | tf_op jit(solution)/shard_map/psum | solution.py:68
Sparse Core Ops, SparseCore 0:
  44.5 33.4 all-reduce.2
  82.5 89.2 all-reduce.4
where the time goes:
time: 182 us; the launch traced here: 181 us
  waiting for transfers between devices  131 us (72%)
  between operations  14.2 us (8%)
  local copies, waits for them, and re-layouts  13.8 us (8%)
  starting transfers between devices  11.7 us (6%)
  other arithmetic  8.56 us (5%)
  matrix products  2.26 us (1%)
    psum x1, waiting for transfers between devices, per_device(): weight_grad = lax.psum(grad_terms, 'node')  89 us
    psum x1, waiting for transfers between devices, per_device(): preact = lax.psum(project(own_rows, averaged, weights), 'feat')  33.6 us
    all_to_all x1, starting transfers between devices, per_device(): lax.all_to_all(request_rows[0], 'node', split_axis=0, concat_axis=0, tile...  7.28 us
    all_to_all x1, waiting for transfers between devices, per_device(): lax.all_to_all(looked, 'node', split_axis=0, concat_axis=0, tiled=True)  6.61 us
    unnamed x8, local copies, waits for them, and re-layouts  5 us
    gather x2, local copies, waits for them, and re-layouts, aggregate(): picked = frontier[local_nbrs]  4.35 us
    all_to_all x1, starting transfers between devices, per_device(): lax.all_to_all(looked, 'node', split_axis=0, concat_axis=0, tiled=True)  4.33 us
  transfers between devices with their start and end apart: 4, of which 4 were waited for; matrix products, arithmetic and copies ran while one was open for 3% of the time, Pallas kernels for 0%

commit v1 on v0

--- a/solution.py
+++ b/solution.py
@@ -1,7 +1,381 @@
+import functools
+
 import jax
 import jax.numpy as jnp
 from jax import lax
+from jax.experimental import pallas as pl
+from jax.experimental.pallas import tpu as pltpu
 from jax.sharding import PartitionSpec as P
+
+MESH = pl.DeviceIdType.MESH
+F32, BF16 = jnp.float32, jnp.bfloat16
+
+
+def matmul(left, right, exact=False):
+    return jnp.dot(
+        left,
+        right,
+        preferred_element_type=F32,
+        precision=lax.Precision.HIGHEST if exact else None,
+    )
+
+
+def step_kernel(
+    sizes,
+    asked_ref,
+    counts_ref,
+    nbrs_ref,
+    nbr_counts_ref,
+    self_ref,
+    table_ref,
+    weights_ref,
+    upstream_ref,
+    hidden_ref,
+    grad_ref,
+    table,
+    upstream,
+    asked,
+    looked,
+    front,
+    proj,
+    hid_out,
+    hid_in,
+    terms,
+    grad,
+    local_sem,
+    ask_send,
+    ask_recv,
+    look_send,
+    look_recv,
+    front_send,
+    front_recv,
+    proj_send,
+    proj_recv,
+    hid_send,
+    hid_recv,
+    term_send,
+    term_recv,
+    out_sem,
+):
+    nodes, feats, caps, fan = sizes
+    slots = nodes * caps
+    depth = nodes // 2
+    portion = hid_in.shape[1]
+    width = hid_in.shape[2]
+    me, mine = lax.axis_index("node"), lax.axis_index("feat")
+    z, y, x, core = me // 2, me % 2, mine // 2, mine % 2
+    node_peers = [lax.rem(me + k, nodes) for k in range(1, nodes)]
+    feat_peers = [lax.rem(mine + k, feats) for k in range(1, feats)]
+    my_columns = pl.ds(pl.multiple_of(mine * width, width), width)
+
+    def columns(index):
+        return pl.ds(pl.multiple_of(index * width, width), width)
+
+    def remote(src, dst, send, recv, node, feat):
+        return pltpu.make_async_remote_copy(
+            src_ref=src,
+            dst_ref=dst,
+            send_sem=send,
+            recv_sem=recv,
+            device_id=(node, feat),
+            device_id_type=MESH,
+        )
+
+    load_table = pltpu.make_async_copy(table_ref, table, local_sem.at[0])
+    load_table.start()
+    load_up = pltpu.make_async_copy(upstream_ref.at[:, my_columns], upstream, local_sem.at[1])
+    load_up.start()
+    load_proj = pltpu.make_async_copy(
+        weights_ref.at[:, :, my_columns], proj.at[mine], local_sem.at[2]
+    )
+    load_proj.start()
+
+    barrier = pltpu.get_barrier_semaphore()
+    for peer in node_peers:
+        pl.semaphore_signal(barrier, inc=1, device_id=(peer, mine), device_id_type=MESH)
+    for peer in feat_peers:
+        pl.semaphore_signal(barrier, inc=1, device_id=(me, peer), device_id_type=MESH)
+
+    targets = nbrs_ref.shape[1]
+    slot = lax.broadcasted_iota(jnp.int32, (slots, targets), 0)
+    owner = jnp.zeros_like(slot)
+    for k in range(1, nodes):
+        owner = owner + (slot >= k * caps).astype(jnp.int32)
+    limit = jnp.zeros_like(slot)
+    for k in range(nodes):
+        limit = jnp.where(owner == k, counts_ref[0, k], limit)
+    live = slot - owner * caps < limit
+    chosen = jnp.where(live & (slot == self_ref[...]), 1.0, 0.0).astype(F32)
+    valid = nbr_counts_ref[...]
+    tally = jnp.zeros((slots, targets), F32)
+    for k in range(fan):
+        tally = tally + jnp.where((slot == nbrs_ref[k : k + 1, :]) & (valid > k), 1.0, 0.0)
+    mean = jnp.where(live, tally / valid.astype(F32), 0.0)
+    chosen_rows = chosen.T.astype(BF16)
+    mean_rows = mean.T
+
+    pl.semaphore_wait(barrier, nodes + feats - 2)
+
+    sends = []
+    for k, peer in enumerate(node_peers):
+        copy = remote(asked_ref.at[peer], asked.at[me], ask_send.at[k], ask_recv.at[me], peer, mine)
+        copy.start()
+        sends.append(copy)
+    for k, peer in enumerate(feat_peers):
+        copy = remote(
+            weights_ref.at[:, :, columns(peer)],
+            proj.at[mine],
+            proj_send.at[k],
+            proj_recv.at[mine],
+            me,
+            peer,
+        )
+        copy.start()
+        sends.append(copy)
+    asked[pl.ds(me, 1)] = asked_ref[pl.ds(me, 1)]
+    for peer in node_peers:
+        remote(asked.at[peer], asked.at[peer], ask_send.at[0], ask_recv.at[peer], peer, mine).wait_recv()
+    wanted = asked[0]
+    for k in range(1, nodes):
+        wanted = wanted + asked[k]
+    load_table.wait()
+    rows = table.shape[1]
+    pick = (lax.broadcasted_iota(jnp.int32, (rows, wanted.shape[1]), 0) == wanted).astype(F32)
+    found = matmul(table[...], pick.astype(BF16)).T
+    looked[pl.ds(me, 1)] = found[:slots].astype(BF16)[None]
+    for k, peer in enumerate(node_peers):
+        copy = remote(looked.at[me], looked.at[me], look_send.at[k], look_recv.at[me], peer, mine)
+        copy.start()
+        sends.append(copy)
+    for peer in node_peers:
+        remote(looked.at[peer], looked.at[peer], look_send.at[0], look_recv.at[peer], peer, mine).wait_recv()
+
+    every = looked[...].reshape(nodes * slots, looked.shape[2])
+
+    def order(requester):
+        row = lax.broadcasted_iota(jnp.int32, (slots, nodes * slots), 0)
+        col = lax.broadcasted_iota(jnp.int32, (slots, nodes * slots), 1)
+        block = jnp.zeros_like(row)
+        for k in range(1, nodes):
+            block = block + (row >= k * caps).astype(jnp.int32)
+        place = block * slots + requester * caps + (row - block * caps)
+        return (col == place).astype(F32).astype(BF16)
+
+    front[pl.ds(mine, 1)] = matmul(order(me), every).astype(BF16)[None]
+    for k, peer in enumerate(feat_peers):
+        copy = remote(front.at[mine], front.at[mine], front_send.at[k], front_recv.at[mine], me, peer)
+        copy.start()
+        sends.append(copy)
+
+    ordered = jnp.concatenate(
+        [matmul(order(r), every).astype(BF16) for r in range(nodes)], axis=0
+    ).T
+
+    def project(index):
+        held = front[pl.ds(index, 1)][0]
+        own_rows = matmul(chosen_rows, held).astype(BF16)
+        averaged = matmul(mean_rows, held.astype(F32), exact=True).astype(BF16)
+        weight = proj[pl.ds(index, 1)][0]
+        return matmul(own_rows, weight[0]) + matmul(averaged, weight[1])
+
+    load_proj.wait()
+    preact = project(mine)
+    for peer in feat_peers:
+        remote(front.at[peer], front.at[peer], front_send.at[0], front_recv.at[peer], me, peer).wait_recv()
+        remote(proj.at[peer], proj.at[peer], proj_send.at[0], proj_recv.at[peer], me, peer).wait_recv()
+        preact = preact + project(peer)
+
+    square = preact * preact
+    bent = jnp.tanh(0.7978845608 * (preact + 0.044715 * preact * square))
+    rise = 0.7978845608 * (1.0 + 3.0 * 0.044715 * square)
+    half = 0.5 * (1.0 + bent)
+    load_up.wait()
+    slope = upstream[...].astype(F32) * (half + 0.5 * preact * (1.0 - bent * bent) * rise)
+    slope = slope.astype(BF16)
+    terms[pl.ds(mine, 1), pl.ds(me, 1), 0:1] = (
+        matmul(chosen.astype(BF16), slope).astype(BF16)[None, None, None]
+    )
+    terms[pl.ds(mine, 1), pl.ds(me, 1), 1:2] = (
+        matmul(mean, slope.astype(F32), exact=True).astype(BF16)[None, None, None]
+    )
+
+    flip_y, flip_x, flip_core = 1 - y, 1 - x, 1 - core
+    depths = [z] + [lax.rem(z + k, depth) for k in range(1, depth)]
+    counter = [0]
+
+    def pass_on(node, feat, to_node, to_feat):
+        copy = remote(
+            terms.at[feat, node],
+            terms.at[feat, node],
+            term_send.at[counter[0]],
+            term_recv.at[feat, node],
+            to_node,
+            to_feat,
+        )
+        counter[0] += 1
+        copy.start()
+        sends.append(copy)
+
+    def arrived(node, feat):
+        remote(
+            terms.at[feat, node],
+            terms.at[feat, node],
+            term_send.at[0],
+            term_recv.at[feat, node],
+            me,
+            2 * x + flip_core,
+        ).wait_recv()
+
+    to_y = (2 * z + flip_y, mine)
+    to_x = (me, 2 * flip_x + core)
+    to_core = (me, 2 * x + flip_core)
+    for k in range(1, depth):
+        pass_on(me, mine, 2 * depths[k] + y, mine)
+    for k in range(depth):
+        node = 2 * depths[k] + y
+        if k > 0:
+            arrived(node, mine)
+        for target in (to_y, to_x, to_core):
+            pass_on(node, mine, *target)
+
+    hid_out[...] = (preact * half).astype(BF16)
+
+    def out_rows(index):
+        return hid_out.at[pl.ds(pl.multiple_of(index * portion, portion), portion), :]
+
+    for k, peer in enumerate(feat_peers):
+        copy = remote(out_rows(peer), hid_in.at[mine], hid_send.at[k], hid_recv.at[mine], me, peer)
+        copy.start()
+        sends.append(copy)
+    hid_in[pl.ds(mine, 1)] = hid_out[pl.ds(pl.multiple_of(mine * portion, portion), portion), :][None]
+
+    across = 2 * flip_x + core
+    early = depth // 2
+    for k in range(depth):
+        node_y, node_x = 2 * depths[k] + flip_y, 2 * depths[k] + y
+        arrived(node_y, mine)
+        if k < early:
+            pass_on(node_y, mine, *to_x)
+        arrived(node_x, across)
+        if k >= early:
+            pass_on(node_x, across, *to_y)
+        pass_on(node_y, mine, *to_core)
+        pass_on(node_x, across, *to_core)
+
+    outs = []
+
+    def gradient(feat, at):
+        held = terms[pl.ds(feat, 1)][0]
+        for layer in range(2):
+            part = held[:, layer].reshape(nodes * slots, width)
+            grad[at, layer] = matmul(ordered, part)
+        copy = pltpu.make_async_copy(
+            grad.at[at], grad_ref.at[:, :, columns(feat)], out_sem.at[at]
+        )
+        copy.start()
+        outs.append(copy)
+
+    gradient(mine, 0)
+    for k in range(depth):
+        node = 2 * depths[k] + flip_y
+        arrived(node, across)
+        pass_on(node, across, *to_core)
+    gradient(across, 1)
+    for at, feat in ((2, 2 * x + flip_core), (3, 2 * flip_x + flip_core)):
+        for node in range(nodes):
+            arrived(node, feat)
+        gradient(feat, at)
+
+    for peer in feat_peers:
+        remote(hid_in.at[peer], hid_in.at[peer], hid_send.at[0], hid_recv.at[peer], me, peer).wait_recv()
+    for k in range(feats):
+        hidden_ref[:, k * width : (k + 1) * width] = hid_in[k]
+    for copy in sends:
+        copy.wait_send()
+    for copy in outs:
+        copy.wait()
+
+
+def compact_step(
+    feature_table,
+    weights,
+    request_rows,
+    request_counts,
+    neighbors,
+    nbr_counts,
+    self_rows,
+    grad_hidden,
+):
+    nodes, feats = lax.axis_size("node"), lax.axis_size("feat")
+    caps, fan = request_rows.shape[2], neighbors.shape[1]
+    slots = nodes * caps
+    targets, hidden = grad_hidden.shape
+    rows, features = feature_table.shape
+    width, portion = hidden // feats, targets // feats
+    me = lax.axis_index("node")
+    lane = jnp.arange(128, dtype=jnp.int32)
+    spread = jnp.pad(jnp.tile(request_rows[0], (1, nodes)), ((0, 0), (0, 128 - slots)))
+    asked = jnp.where(lane[None, :] // caps == me, spread, 0).reshape(nodes, 1, 128)
+    dma = pltpu.SemaphoreType.DMA
+    vmem = pl.BlockSpec(memory_space=pltpu.VMEM)
+    anywhere = pl.BlockSpec(memory_space=pl.ANY)
+    moves = 2 * nodes * feats
+    return pl.pallas_call(
+        functools.partial(step_kernel, (nodes, feats, caps, fan)),
+        out_shape=(
+            jax.ShapeDtypeStruct((portion, hidden), BF16),
+            jax.ShapeDtypeStruct((2, features, hidden), F32),
+        ),
+        in_specs=[
+            vmem,
+            pl.BlockSpec(memory_space=pltpu.SMEM),
+            vmem,
+            vmem,
+            vmem,
+            anywhere,
+            anywhere,
+            anywhere,
+        ],
+        out_specs=(vmem, anywhere),
+        scratch_shapes=[
+            pltpu.VMEM((features, rows), BF16),
+            pltpu.VMEM((targets, width), BF16),
+            pltpu.VMEM((nodes, 1, 128), jnp.int32),
+            pltpu.VMEM((nodes, slots, features), BF16),
+            pltpu.VMEM((feats, slots, features), BF16),
+            pltpu.VMEM((feats, 2, features, width), BF16),
+            pltpu.VMEM((targets, width), BF16),
+            pltpu.VMEM((feats, portion, width), BF16),
+            pltpu.VMEM((feats, nodes, 2, slots, width), BF16),
+            pltpu.VMEM((feats, 2, features, width), F32),
+            dma((3,)),
+            dma((nodes,)),
+            dma((nodes,)),
+            dma((nodes,)),
+            dma((nodes,)),
+            dma((feats,)),
+            dma((feats,)),
+            dma((feats,)),
+            dma((feats,)),
+            dma((feats,)),
+            dma((feats,)),
+            dma((moves,)),
+            dma((feats, nodes)),
+            dma((feats,)),
+        ],
+        compiler_params=pltpu.CompilerParams(
+            collective_id=0, has_side_effects=True, vmem_limit_bytes=32 * 1024 * 1024
+        ),
+    )(
+        asked,
+        request_counts,
+        neighbors.T,
+        nbr_counts[None],
+        self_rows[None],
+        feature_table.T,
+        weights,
+        grad_hidden,
+    )
 
 
 def smooth_gate(values):
@@ -80,8 +454,17 @@
         P("node"),
         P("node", None),
     )
+    nodes, feats = mesh.shape["node"], mesh.shape["feat"]
+
+    def per_slice(feature_table, weights, request_rows, *others):
+        slots = nodes * request_rows.shape[2]
+        plan = per_device
+        if feats == 4 and nodes % 2 == 0 and slots % 16 == 0 and slots <= 128:
+            plan = compact_step
+        return plan(feature_table, weights, request_rows, *others)
+
     return jax.shard_map(
-        per_device,
+        per_slice,
         mesh=mesh,
         in_specs=placed,
         out_specs=(P(("node", "feat"), None), P(None, "feat", None)),

time: 182 us -> 47 us (0.26)
  waiting for transfers between devices: 131 us -> 0 us
  Pallas kernels: 0 us -> 37.1 us
  between operations: 14.2 us -> 0.66 us
  starting transfers between devices: 11.7 us -> 0 us
  other arithmetic: 8.56 us -> 0.02 us
  local copies, waits for them, and re-layouts: 13.8 us -> 8.65 us
  matrix products: 2.26 us -> 0 us
    psum x2 -> x0, waiting for transfers between devices: 123 us -> none  [the longest x1 89 us: per_device(): weight_grad = lax.psum(grad_terms, 'node')]
    pallas_call x0 -> x1, Pallas kernels: none -> 37.1 us  [compact_step(): pl.pallas_call(functools.partial(step_kernel, (nodes, feats, caps, fan)),...]
    all_to_all x2 -> x0, starting transfers between devices: 11.6 us -> none  [the longest x1 7.28 us: per_device(): lax.all_to_all(request_rows[0], 'node', split_axis=0, concat_axis=0, tile...]
    all_to_all x2 -> x0, waiting for transfers between devices: 8.29 us -> none  [the longest x1 6.61 us: per_device(): lax.all_to_all(looked, 'node', split_axis=0, concat_axis=0, tiled=True)]
    gather x5 -> x0, local copies, waits for them, and re-layouts: 6.8 us -> none  [the longest x2 4.35 us: aggregate(): picked = frontier[local_nbrs]]
    unnamed x8 -> x17, local copies, waits for them, and re-layouts: 5 us -> 8.57 us
    convert_element_type x3 -> x0, other arithmetic: 2.83 us -> none  [the longest x2 2.83 us: activate(): return (output.astype(jnp.bfloat16), slope.astype(jnp.bfloat16))]
    dot_general x4 -> x0, matrix products: 2.26 us -> none  [the longest x1 1.32 us: project(): jnp.dot(averaged, weights[1], preferred_element_type=jnp.float32)]
  transfers between devices with their start and end apart: 4 -> 0, of which waited for: 4 -> 0; matrix products, arithmetic and copies ran while one was open for 3% -> 0% of each run, Pallas kernels for 0% -> 0%
where the time goes in v1:
time: 47 us; the launch traced here: 46.5 us
  Pallas kernels  37.1 us (79%)
  local copies, waits for them, and re-layouts  8.65 us (18%)
  between operations  0.66 us (1%)
    pallas_call x1, Pallas kernels, compact_step(): pl.pallas_call(functools.partial(step_kernel, (nodes, feats, caps, fan)),...  37.1 us
    unnamed x17, local copies, waits for them, and re-layouts  8.57 us

profile of v1, /device:TPU:0, one launch (start us, length us, event | category | flops | bytes accessed | tf_op | source)
XLA Modules:
  0.0 46.5 jit_solution(12212537426443896273)
XLA Ops:
  0.7 0.8 %copy.11 = s32[1,8,6]{2,1,0:T(8,128)S(1)} copy(s32[1,8,6]{1,0,2:T(1,128)} %param.10) | data formatting | bytes 384 | tf_op args[2]
  1.4 0.1 tile.12
  1.5 0.0 copy-start
  1.5 1.1 %copy-done = bf16[2048,192]{0,1:T(8,128)(2,1)S(1)} copy-done((bf16[2048,192]{0,1:T(8,128)(2,1)S(1)}, bf16[2048,192]{0,1:T(8,128)(2,1)}, u32[]{:S(2)}) %copy-start) | copy-done | bytes 786456
  2.6 0.0 copy-start.1
  2.6 1.1 %copy-done.1 = bf16[2,192,1024]{2,1,0:T(8,128)(2,1)S(1)} copy-done((bf16[2,192,1024]{2,1,0:T(8,128)(2,1)S(1)}, bf16[2,192,1024]{2,1,0:T(8,128)(2,1)}, u32[]{:S(2)}) %copy-start.1) | copy-done | bytes 786456
  3.8 0.0 copy-start.2
  3.8 1.0 %copy-done.2 = bf16[256,1024]{1,0:T(8,128)(2,1)S(1)} copy-done((bf16[256,1024]{1,0:T(8,128)(2,1)S(1)}, bf16[256,1024]{1,0:T(8,128)(2,1)}, u32[]{:S(2)}) %copy-start.2) | copy-done | bytes 524312
  4.8 0.0 copy-start.3
  4.8 0.7 %copy-done.3 = s32[256,5]{0,1:T(8,128)S(1)} copy-done((s32[256,5]{0,1:T(8,128)S(1)}, s32[256,5]{0,1:T(8,128)}, u32[]{:S(2)}) %copy-start.3) | copy-done | bytes 5144
  5.5 0.0 copy-start.4
  5.5 0.7 %copy-done.4 = s32[256]{0:T(256)S(1)} copy-done((s32[256]{0:T(256)S(1)}, s32[256]{0:T(256)}, u32[]{:S(2)}) %copy-start.4) | copy-done | bytes 1048
  6.2 0.0 copy-start.5
  6.2 0.7 %copy-done.5 = s32[256]{0:T(256)S(1)} copy-done((s32[256]{0:T(256)S(1)}, s32[256]{0:T(256)}, u32[]{:S(2)}) %copy-start.5) | copy-done | bytes 1048
  6.9 0.0 copy-start.6
  6.9 0.7 %copy-done.6 = s32[1,8]{1,0:T(1,128)S(1)} copy-done((s32[1,8]{1,0:T(1,128)S(1)}, s32[1,8]{1,0:T(1,128)}, u32[]{:S(2)}) %copy-start.6) | copy-done | bytes 56
  7.5 37.1 %shard_map.95 = (bf16[64,1024]{1,0:T(8,128)(2,1)S(1)}, f32[2,192,1024]{2,1,0:T(8,128)S(1)}) custom-call(s32[8,1,128]{2,1,0:T(1,128)S(1)} %bitcast.7, s32[1,8]{1,0:T(1,128)S(1)} %copy-done.6, s32[5,256]{1,0:T(8,128)S(1)} %bitcast.8, s32[1,256]{1,0:T(1,128)S(1)} %bitcast.9, s32[1,256]{1,0:T(1,128)S(1)} %bitcast.10, bf16[192,2048]{1,0:T(8,128)(2,1)S(1)} %bitcast.6, ...), custom_call_target="tpu_custom_call" | custom-call | tf_op jit(solution)/shard_map/pallas_call | solution.py:323
  44.7 0.7 %copy.14 = bf16[64,1024]{1,0:T(8,128)(2,1)} copy(bf16[64,1024]{1,0:T(8,128)(2,1)S(1)} %get-tuple-element.4) | data formatting | bytes 262144
  45.3 1.1 %copy.15 = f32[2,192,1024]{2,1,0:T(8,128)} copy(f32[2,192,1024]{2,1,0:T(8,128)S(1)} %get-tuple-element.5) | data formatting | bytes 3145728
  (3 shorter events, 0.0 us)
Async XLA Ops:
  1.5 1.1 %copy-start = (bf16[2048,192]{0,1:T(8,128)(2,1)S(1)}, bf16[2048,192]{0,1:T(8,128)(2,1)}, u32[]{:S(2)}) copy-start(bf16[2048,192]{0,1:T(8,128)(2,1)} %param.8) | copy-start | bytes 2359300
  2.6 1.1 %copy-start.1 = (bf16[2,192,1024]{2,1,0:T(8,128)(2,1)S(1)}, bf16[2,192,1024]{2,1,0:T(8,128)(2,1)}, u32[]{:S(2)}) copy-start(bf16[2,192,1024]{2,1,0:T(8,128)(2,1)} %weights_ref.1) | copy-start | bytes 2359300
  3.8 1.0 %copy-start.2 = (bf16[256,1024]{1,0:T(8,128)(2,1)S(1)}, bf16[256,1024]{1,0:T(8,128)(2,1)}, u32[]{:S(2)}) copy-start(bf16[256,1024]{1,0:T(8,128)(2,1)} %upstream_ref.1) | copy-start | bytes 1572868
  4.8 0.7 %copy-start.3 = (s32[256,5]{0,1:T(8,128)S(1)}, s32[256,5]{0,1:T(8,128)}, u32[]{:S(2)}) copy-start(s32[256,5]{0,1:T(8,128)} %param.12) | copy-start | bytes 15364
  5.5 0.7 %copy-start.4 = (s32[256]{0:T(256)S(1)}, s32[256]{0:T(256)}, u32[]{:S(2)}) copy-start(s32[256]{0:T(256)} %param.13) | copy-start | bytes 3076
  6.2 0.7 %copy-start.5 = (s32[256]{0:T(256)S(1)}, s32[256]{0:T(256)}, u32[]{:S(2)}) copy-start(s32[256]{0:T(256)} %param.14) | copy-start | bytes 3076
  6.9 0.7 %copy-start.6 = (s32[1,8]{1,0:T(1,128)S(1)}, s32[1,8]{1,0:T(1,128)}, u32[]{:S(2)}) copy-start(s32[1,8]{1,0:T(1,128)} %counts_ref.1) | copy-start | bytes 100

commit v2 on v1

v2 whole, which is shorter than its diff:
```python
import functools

import jax
import jax.numpy as jnp
from jax import lax
from jax.experimental import pallas as pl
from jax.experimental.pallas import tpu as pltpu
from jax.sharding import PartitionSpec as P

MESH = pl.DeviceIdType.MESH
F32, BF16 = jnp.float32, jnp.bfloat16


def matmul(left, right):
    return jnp.dot(left, right, preferred_element_type=F32)


def step_kernel(
    sizes,
    request_ref,
    counts_ref,
    nbrs_ref,
    nbr_counts_ref,
    self_ref,
    table_ref,
    weights_ref,
    upstream_ref,
    hidden_ref,
    terms,
    ordered_ref,
    request,
    counts,
    nbrs,
    nbr_counts,
    self_rows,
    table,
    upstream,
    ask_out,
    asked,
    stacked,
    looked,
    front,
    proj,
    preact_ref,
    hid_out,
    own_terms,
    in_order,
    local_sem,
    ask_send,
    ask_recv,
    look_send,
    look_recv,
    front_send,
    front_recv,
    proj_send,
    proj_recv,
    hid_send,
    hid_recv,
    term_send,
    term_recv,
):
    nodes, feats, caps, fan = sizes
    slots = nodes * caps
    depth = nodes // 2
    portion = hidden_ref.shape[1]
    width = hidden_ref.shape[2]
    me, mine = lax.axis_index("node"), lax.axis_index("feat")
    z, y, x, core = me // 2, me % 2, mine // 2, mine % 2
    node_peers = [lax.rem(me + k, nodes) for k in range(1, nodes)]
    feat_peers = [lax.rem(mine + k, feats) for k in range(1, feats)]
    my_columns = pl.ds(pl.multiple_of(mine * width, width), width)

    def columns(index):
        return pl.ds(pl.multiple_of(index * width, width), width)

    def remote(src, dst, send, recv, node, feat):
        return pltpu.make_async_remote_copy(
            src_ref=src,
            dst_ref=dst,
            send_sem=send,
            recv_sem=recv,
            device_id=(node, feat),
            device_id_type=MESH,
        )

    loads = []
    for k, (src, dst) in enumerate(
        (
            (request_ref, request),
            (nbrs_ref, nbrs),
            (nbr_counts_ref, nbr_counts),
            (self_ref, self_rows),
            (counts_ref, counts),
            (table_ref, table),
            (weights_ref.at[:, :, my_columns], proj.at[mine]),
            (upstream_ref.at[:, my_columns], upstream),
        )
    ):
        copy = pltpu.make_async_copy(src, dst, local_sem.at[k])
        copy.start()
        loads.append(copy)

    barrier = pltpu.get_barrier_semaphore()
    for peer in node_peers:
        pl.semaphore_signal(barrier, inc=1, device_id=(peer, mine), device_id_type=MESH)
    for peer in feat_peers:
        pl.semaphore_signal(barrier, inc=1, device_id=(me, peer), device_id_type=MESH)

    ask_out[...] = jnp.zeros_like(ask_out)
    loads[0].wait()
    for k in range(caps):
        ask_out[k : k + 1, 0:nodes] = request[k]
    pl.semaphore_wait(barrier, nodes + feats - 2)

    sends = []
    for k, peer in enumerate(node_peers):
        copy = remote(ask_out, asked.at[me], ask_send.at[k], ask_recv.at[me], peer, mine)
        copy.start()
        sends.append(copy)
    for k, peer in enumerate(feat_peers):
        copy = remote(
            weights_ref.at[:, :, columns(peer)],
            proj.at[mine],
            proj_send.at[k],
            proj_recv.at[mine],
            me,
            peer,
        )
        copy.start()
        sends.append(copy)
    asked[pl.ds(me, 1)] = ask_out[...][None]

    for copy in loads[1:5]:
        copy.wait()
    targets = nbrs.shape[1]

    def owner_of(slot):
        owner = jnp.zeros_like(slot)
        for k in range(1, nodes):
            owner = owner + (slot >= k * caps).astype(jnp.int32)
        return owner

    held_by = owner_of(lax.broadcasted_iota(jnp.int32, (slots, nodes), 0))
    here = lax.broadcasted_iota(jnp.int32, (slots, nodes), 1) == held_by
    limit = jnp.sum(
        jnp.where(here, counts[...].astype(F32), 0.0), axis=1, keepdims=True
    )
    slot = lax.broadcasted_iota(jnp.int32, (slots, targets), 0)
    live = (slot - owner_of(slot) * caps).astype(F32) < limit
    chosen = jnp.where(live & (slot == self_rows[...]), 1.0, 0.0).astype(F32)
    valid = nbr_counts[...]
    tally = jnp.zeros((slots, targets), F32)
    for k in range(fan):
        tally = tally + jnp.where((slot == nbrs[k : k + 1, :]) & (valid > k), 1.0, 0.0)
    tally = jnp.where(live, tally, 0.0)
    share = 1.0 / valid.astype(F32)
    mean = tally * share
    mean_high = mean.astype(BF16)
    mean_low = (mean - mean_high.astype(F32)).astype(BF16)
    back = jnp.concatenate([chosen.astype(BF16), mean_high, mean_low], axis=0)
    chosen_rows = chosen.T.astype(BF16)
    tally_rows = tally.T.astype(BF16)
    share_rows = jnp.broadcast_to(share, (128, targets)).T[:, 0:1]

    for peer in node_peers:
        remote(asked.at[peer], asked.at[peer], ask_send.at[0], ask_recv.at[peer], peer, mine).wait_recv()
    for r in range(nodes):
        stacked[r * caps : (r + 1) * caps, :] = asked[r, 0:caps, :]
    lane = lax.broadcasted_iota(jnp.int32, stacked.shape, 1)
    wanted = jnp.sum(
        jnp.where(lane == me, stacked[...].astype(F32), 0.0), axis=1, keepdims=True
    ).astype(jnp.int32)
    rows = table.shape[1]
    pick = (lax.broadcasted_iota(jnp.int32, (slots, rows), 1) == wanted).astype(F32)
    loads[5].wait()
    found = lax.dot_general(
        pick.astype(BF16), table[...], (((1,), (1,)), ((), ())), preferred_element_type=F32
    )
    looked[pl.ds(me, 1)] = found.astype(BF16)[None]
    for k, peer in enumerate(node_peers):
        copy = remote(looked.at[me], looked.at[me], look_send.at[k], look_recv.at[me], peer, mine)
        copy.start()
        sends.append(copy)
    for peer in node_peers:
        remote(looked.at[peer], looked.at[peer], look_send.at[0], look_recv.at[peer], peer, mine).wait_recv()

    every = looked[...].reshape(nodes * slots, looked.shape[2])

    def order(requester):
        row = lax.broadcasted_iota(jnp.int32, (slots, nodes * slots), 0)
        col = lax.broadcasted_iota(jnp.int32, (slots, nodes * slots), 1)
        block = owner_of(row)
        place = block * slots + requester * caps + (row - block * caps)
        return (col == place).astype(F32).astype(BF16)

    front[pl.ds(mine, 1)] = matmul(order(me), every).astype(BF16)[None]
    for k, peer in enumerate(feat_peers):
        copy = remote(front.at[mine], front.at[mine], front_send.at[k], front_recv.at[mine], me, peer)
        copy.start()
        sends.append(copy)

    @pl.loop(0, nodes)
    def _(r):
        start = pl.multiple_of(r * slots, slots)
        in_order[pl.ds(start, slots), :] = matmul(order(r), every).astype(BF16)

    ordered_ref[...] = in_order[...].T

    loads[6].wait()
    preact_ref[...] = jnp.zeros_like(preact_ref)

    @pl.loop(0, feats)
    def _(k):
        index = lax.rem(mine + k, feats)

        @pl.when(k > 0)
        def _():
            remote(front.at[index], front.at[index], front_send.at[0], front_recv.at[index], me, index).wait_recv()
            remote(proj.at[index], proj.at[index], proj_send.at[0], proj_recv.at[index], me, index).wait_recv()

        held = front[pl.ds(index, 1)][0]
        own_rows = matmul(chosen_rows, held).astype(BF16)
        averaged = (matmul(tally_rows, held) * share_rows).astype(BF16)
        weight = proj[pl.ds(index, 1)][0]
        preact_ref[...] += matmul(own_rows, weight[0]) + matmul(averaged, weight[1])

    preact = preact_ref[...]
    square = preact * preact
    bent = jnp.tanh(0.7978845608 * (preact + 0.044715 * preact * square))
    rise = 0.7978845608 * (1.0 + 3.0 * 0.044715 * square)
    half = 0.5 * (1.0 + bent)
    loads[7].wait()
    slope = upstream[...].astype(F32) * (half + 0.5 * preact * (1.0 - bent * bent) * rise)
    both = matmul(back, slope.astype(BF16))
    own_terms[0] = both[:slots].astype(BF16)
    own_terms[1] = (both[slots : 2 * slots] + both[2 * slots :]).astype(BF16)
    keep = pltpu.make_async_copy(own_terms, terms.at[mine, me], local_sem.at[8])
    keep.start()

    flip_y, flip_x, flip_core = 1 - y, 1 - x, 1 - core
    depths = [z] + [lax.rem(z + k, depth) for k in range(1, depth)]
    counter = [0]

    def pass_on(node, feat, to_node, to_feat, src=None):
        copy = remote(
            terms.at[feat, node] if src is None else src,
            terms.at[feat, node],
            term_send.at[counter[0]],
            term_recv.at[feat, node],
            to_node,
            to_feat,
        )
        counter[0] += 1
        copy.start()
        sends.append(copy)

    def arrived(node, feat):
        remote(
            terms.at[feat, node],
            terms.at[feat, node],
            term_send.at[0],
            term_recv.at[feat, node],
            me,
            2 * x + flip_core,
        ).wait_recv()

    to_y = (2 * z + flip_y, mine)
    to_x = (me, 2 * flip_x + core)
    to_core = (me, 2 * x + flip_core)
    for k in range(1, depth):
        pass_on(me, mine, 2 * depths[k] + y, mine, own_terms)
    for k in range(depth):
        node = 2 * depths[k] + y
        if k > 0:
            arrived(node, mine)
        for target in (to_y, to_x, to_core):
            pass_on(node, mine, *target, src=own_terms if k == 0 else None)

    hid_out[...] = (preact * half).astype(BF16)

    def out_rows(index):
        return hid_out.at[pl.ds(pl.multiple_of(index * portion, portion), portion), :]

    for k, peer in enumerate(feat_peers):
        copy = remote(out_rows(peer), hidden_ref.at[mine], hid_send.at[k], hid_recv.at[mine], me, peer)
        copy.start()
        sends.append(copy)
    keep_rows = pltpu.make_async_copy(out_rows(mine), hidden_ref.at[mine], local_sem.at[9])
    keep_rows.start()

    across = 2 * flip_x + core
    early = depth // 2
    for k in range(depth):
        node_y, node_x = 2 * depths[k] + flip_y, 2 * depths[k] + y
        arrived(node_y, mine)
        if k < early:
            pass_on(node_y, mine, *to_x)
        arrived(node_x, across)
        if k >= early:
            pass_on(node_x, across, *to_y)
        pass_on(node_y, mine, *to_core)
        pass_on(node_x, across, *to_core)

    for k in range(depth):
        node = 2 * depths[k] + flip_y
        arrived(node, across)
        pass_on(node, across, *to_core)
    for feat in (2 * x + flip_core, 2 * flip_x + flip_core):
        for node in range(nodes):
            arrived(node, feat)
    for peer in feat_peers:
        remote(hidden_ref.at[peer], hidden_ref.at[peer], hid_send.at[0], hid_recv.at[peer], me, peer).wait_recv()
    for copy in sends:
        copy.wait_send()
    keep.wait()
    keep_rows.wait()


def gradient_kernel(hidden_in, terms, ordered, hidden_ref, grad_ref, rows_out, grad, out_sem):
    feats, nodes, layers, slots, width = terms.shape
    for k in range(feats):
        rows_out[:, k * width : (k + 1) * width] = hidden_in[k]
    keep_rows = pltpu.make_async_copy(rows_out, hidden_ref, out_sem.at[feats])
    keep_rows.start()

    def part(feat):
        columns = pl.ds(pl.multiple_of(feat * width, width), width)
        return pltpu.make_async_copy(grad.at[feat], grad_ref.at[:, :, columns], out_sem.at[feat])

    @pl.loop(0, feats)
    def _(feat):
        held = terms[pl.ds(feat, 1)][0]
        for layer in range(layers):
            total = matmul(ordered[...], held[:, layer].reshape(nodes * slots, width))
            grad[pl.ds(feat, 1), layer : layer + 1] = total[None, None]
        part(feat).start()

    @pl.loop(0, feats)
    def _(feat):
        part(feat).wait()

    keep_rows.wait()


def compact_step(
    feature_table,
    weights,
    request_rows,
    request_counts,
    neighbors,
    nbr_counts,
    self_rows,
    grad_hidden,
):
    nodes, feats = lax.axis_size("node"), lax.axis_size("feat")
    caps, fan = request_rows.shape[2], neighbors.shape[1]
    slots = nodes * caps
    targets, hidden = grad_hidden.shape
    rows, features = feature_table.shape
    width, portion = hidden // feats, targets // feats
    dma = pltpu.SemaphoreType.DMA
    vmem = pl.BlockSpec(memory_space=pltpu.VMEM)
    anywhere = pl.BlockSpec(memory_space=pl.ANY)
    moves = nodes * feats - 1
    hidden_in, terms, ordered = pl.pallas_call(
        functools.partial(step_kernel, (nodes, feats, caps, fan)),
        out_shape=(
            jax.ShapeDtypeStruct((feats, portion, width), BF16),
            jax.ShapeDtypeStruct((feats, nodes, 2, slots, width), BF16),
            jax.ShapeDtypeStruct((features, nodes * slots), BF16),
        ),
        in_specs=[pl.BlockSpec(memory_space=pltpu.HBM)] * 8,
        out_specs=(anywhere, anywhere, vmem),
        scratch_shapes=[
            pltpu.VMEM((caps, 1, nodes), jnp.int32),
            pltpu.VMEM((1, nodes), jnp.int32),
            pltpu.VMEM((fan, targets), jnp.int32),
            pltpu.VMEM((1, targets), jnp.int32),
            pltpu.VMEM((1, targets), jnp.int32),
            pltpu.VMEM((features, rows), BF16),
            pltpu.VMEM((targets, width), BF16),
            pltpu.VMEM((8, 128), jnp.int32),
            pltpu.VMEM((nodes, 8, 128), jnp.int32),
            pltpu.VMEM((slots, 128), jnp.int32),
            pltpu.VMEM((nodes, slots, features), BF16),
            pltpu.VMEM((feats, slots, features), BF16),
            pltpu.VMEM((feats, 2, features, width), BF16),
            pltpu.VMEM((targets, width), F32),
            pltpu.VMEM((targets, width), BF16),
            pltpu.VMEM((2, slots, width), BF16),
            pltpu.VMEM((nodes * slots, features), BF16),
            dma((10,)),
            dma((nodes,)),
            dma((nodes,)),
            dma((nodes,)),
            dma((nodes,)),
            dma((feats,)),
            dma((feats,)),
            dma((feats,)),
            dma((feats,)),
            dma((feats,)),
            dma((feats,)),
            dma((moves,)),
            dma((feats, nodes)),
        ],
        compiler_params=pltpu.CompilerParams(
            collective_id=0, has_side_effects=True, vmem_limit_bytes=24 * 1024 * 1024
        ),
    )(
        request_rows.transpose(2, 0, 1),
        request_counts,
        neighbors.T,
        nbr_counts[None],
        self_rows[None],
        feature_table.T,
        weights,
        grad_hidden,
    )
    hbm = pl.BlockSpec(memory_space=pltpu.HBM)
    return pl.pallas_call(
        gradient_kernel,
        out_shape=(
            jax.ShapeDtypeStruct((portion, hidden), BF16),
            jax.ShapeDtypeStruct((2, features, hidden), F32),
        ),
        in_specs=[vmem, vmem, vmem],
        out_specs=(hbm, hbm),
        scratch_shapes=[
            pltpu.VMEM((portion, hidden), BF16),
            pltpu.VMEM((feats, 2, features, width), F32),
            dma((feats + 1,)),
        ],
        compiler_params=pltpu.CompilerParams(vmem_limit_bytes=24 * 1024 * 1024),
    )(hidden_in, terms, ordered)


def smooth_gate(values):
    return (
        0.5
        * values
        * (1.0 + jnp.tanh(0.7978845608 * (values + 0.044715 * values * values * values)))
    )


def activate(preact, upstream):
    output, pullback = jax.vjp(smooth_gate, preact)
    slope = pullback(upstream.astype(jnp.float32))[0]
    return (output.astype(jnp.bfloat16), slope.astype(jnp.bfloat16))


def aggregate(frontier, local_nbrs, local_counts):
    picked = frontier[local_nbrs]
    within = jnp.arange(local_nbrs.shape[1], dtype=jnp.int32)[None, :] < local_counts[:, None]
    summed = jnp.sum(
        jnp.where(within[:, :, None], picked, jnp.zeros_like(picked)), axis=1, dtype=jnp.float32
    )
    return (summed / local_counts[:, None].astype(jnp.float32)).astype(jnp.bfloat16)


def project(own_rows, averaged, weights):
    first = jnp.dot(own_rows, weights[0], preferred_element_type=jnp.float32)
    return first + jnp.dot(averaged, weights[1], preferred_element_type=jnp.float32)


def contract(left_side, right_side):
    return lax.dot_general(
        left_side, right_side, (((0,), (0,)), ((), ())), preferred_element_type=jnp.float32
    )


def per_device(
    feature_table,
    weights,
    request_rows,
    request_counts,
    neighbors,
    nbr_counts,
    self_rows,
    grad_hidden,
):
    slot_count = request_rows.shape[2]
    looked = feature_table[
        lax.all_to_all(request_rows[0], "node", split_axis=0, concat_axis=0, tiled=True)
    ]
    fetched = lax.all_to_all(looked, "node", split_axis=0, concat_axis=0, tiled=True)
    filled = jnp.arange(slot_count, dtype=jnp.int32)[None, :] < request_counts[0][:, None]
    frontier = jnp.where(filled[:, :, None], fetched, jnp.zeros_like(fetched)).reshape(
        -1, fetched.shape[2]
    )
    own_rows = frontier[self_rows]
    averaged = aggregate(frontier, neighbors, nbr_counts)
    groups = lax.axis_size("feat")
    portion = own_rows.shape[0] // groups
    preact = lax.psum(project(own_rows, averaged, weights), "feat")
    output_all, slope = activate(preact, grad_hidden)
    hidden = lax.dynamic_slice_in_dim(output_all, lax.axis_index("feat") * portion, portion, 0)
    grad_terms = jnp.stack([contract(own_rows, slope), contract(averaged, slope)])
    weight_grad = lax.psum(grad_terms, "node")
    return (hidden, weight_grad)


def solution(mesh):
    placed = (
        P("node", "feat"),
        P(None, "feat", None),
        P("node", None, None),
        P("node", None),
        P("node", None),
        P("node"),
        P("node"),
        P("node", None),
    )
    nodes, feats = mesh.shape["node"], mesh.shape["feat"]

    def per_slice(feature_table, weights, request_rows, *others):
        slots = nodes * request_rows.shape[2]
        plan = per_device
        if feats == 4 and nodes % 2 == 0 and slots % 16 == 0 and slots <= 128 and request_rows.shape[2] <= 8:
            plan = compact_step
        return plan(feature_table, weights, request_rows, *others)

    return jax.shard_map(
        per_slice,
        mesh=mesh,
        in_specs=placed,
        out_specs=(P(("node", "feat"), None), P(None, "feat", None)),
        check_vma=False,
    )
```

time: 47 us -> 45 us (0.957)
  local copies, waits for them, and re-layouts: 8.65 us -> 6.69 us
    unnamed x17 -> x16, local copies, waits for them, and re-layouts: 8.57 us -> 6.69 us
    pallas_call x0 -> x1, Pallas kernels: none -> 1.86 us  [compact_step(): pl.pallas_call(gradient_kernel, out_shape=(jax.ShapeDtypeStruct((portion,...]
    pallas_call x1, Pallas kernels: 37.1 us -> 35.4 us  [compact_step(): pl.pallas_call(functools.partial(step_kernel, (nodes, feats, caps, fan)),...]
where the time goes in v2:
time: 45 us; the launch traced here: 44.6 us
  Pallas kernels  37.2 us (83%)
  local copies, waits for them, and re-layouts  6.69 us (15%)
  between operations  0.66 us (1%)
    pallas_call x1, Pallas kernels, compact_step(): pl.pallas_call(functools.partial(step_kernel, (nodes, feats, caps, fan)),...  35.4 us
    unnamed x16, local copies, waits for them, and re-layouts  6.69 us
    pallas_call x1, Pallas kernels, compact_step(): pl.pallas_call(gradient_kernel, out_shape=(jax.ShapeDtypeStruct((portion,...  1.86 us

profile of v2, /device:TPU:0, one launch (start us, length us, event | category | flops | bytes accessed | tf_op | source)
XLA Modules:
  0.0 44.6 jit_solution(4044199162967882971)
XLA Ops:
  0.6 0.0 copy-start
  0.6 1.1 %copy-done = bf16[2048,192]{0,1:T(8,128)(2,1)S(1)} copy-done((bf16[2048,192]{0,1:T(8,128)(2,1)S(1)}, bf16[2048,192]{0,1:T(8,128)(2,1)}, u32[]{:S(2)}) %copy-start) | copy-done | bytes 786456
  1.8 0.0 copy-start.1
  1.8 1.1 %copy-done.1 = bf16[2,192,1024]{2,1,0:T(8,128)(2,1)S(1)} copy-done((bf16[2,192,1024]{2,1,0:T(8,128)(2,1)S(1)}, bf16[2,192,1024]{2,1,0:T(8,128)(2,1)}, u32[]{:S(2)}) %copy-start.1) | copy-done | bytes 786456
  2.9 0.0 copy-start.2
  2.9 1.0 %copy-done.2 = bf16[256,1024]{1,0:T(8,128)(2,1)S(1)} copy-done((bf16[256,1024]{1,0:T(8,128)(2,1)S(1)}, bf16[256,1024]{1,0:T(8,128)(2,1)}, u32[]{:S(2)}) %copy-start.2) | copy-done | bytes 524312
  3.9 0.0 copy-start.3
  3.9 0.7 %copy-done.3 = s32[256,5]{0,1:T(8,128)S(1)} copy-done((s32[256,5]{0,1:T(8,128)S(1)}, s32[256,5]{0,1:T(8,128)}, u32[]{:S(2)}) %copy-start.3) | copy-done | bytes 5144
  4.6 0.0 copy-start.4
  4.6 0.7 %copy-done.4 = s32[1,8,6]{1,0,2:T(1,128)S(1)} copy-done((s32[1,8,6]{1,0,2:T(1,128)S(1)}, s32[1,8,6]{1,0,2:T(1,128)}, u32[]{:S(2)}) %copy-start.4) | copy-done | bytes 216
  5.3 0.0 copy-start.5
  5.3 0.7 %copy-done.5 = s32[256]{0:T(256)S(1)} copy-done((s32[256]{0:T(256)S(1)}, s32[256]{0:T(256)}, u32[]{:S(2)}) %copy-start.5) | copy-done | bytes 1048
  6.0 0.0 copy-start.6
  6.0 0.7 %copy-done.6 = s32[256]{0:T(256)S(1)} copy-done((s32[256]{0:T(256)S(1)}, s32[256]{0:T(256)}, u32[]{:S(2)}) %copy-start.6) | copy-done | bytes 1048
  6.7 0.0 copy-start.7
  6.7 0.7 %copy-done.7 = s32[1,8]{1,0:T(1,128)S(1)} copy-done((s32[1,8]{1,0:T(1,128)S(1)}, s32[1,8]{1,0:T(1,128)}, u32[]{:S(2)}) %copy-start.7) | copy-done | bytes 56
  7.3 35.4 %shard_map.95 = (bf16[4,64,256]{2,1,0:T(8,128)(2,1)S(1)}, bf16[4,8,2,48,256]{4,3,2,1,0:T(8,128)(2,1)S(1)}, bf16[192,384]{1,0:T(8,128)(2,1)S(1)}) custom-call(s32[6,1,8]{2,1,0:T(1,128)S(1)} %bitcast.7, s32[1,8]{1,0:T(1,128)S(1)} %copy-done.7, s32[5,256]{1,0:T(8,128)S(1)} %bitcast.6, s32[1,256]{1,0:T(1,128)S(1)} %bitcast.8, s32[1,256]{1,0:T(1,128)S(1)} %bitcast.9, ...), custom_call_target="tpu_custom_call" | custom-call | tf_op jit(solution)/shard_map/pallas_call | solution.py:365
  42.7 1.9 %shard_map.96 = (bf16[64,1024]{1,0:T(8,128)(2,1)}, f32[2,192,1024]{2,1,0:T(8,128)}) custom-call(bf16[4,64,256]{2,1,0:T(8,128)(2,1)S(1)} %get-tuple-element.5.hidden_in, bf16[4,8,2,48,256]{4,3,2,1,0:T(8,128)(2,1)S(1)} %get-tuple-element.6.terms, bf16[192,384]{1,0:T(8,128)(2,1)S(1)} %get-tuple-element.7.ordered), custom_call_target="tpu_custom_call" | custom-call | tf_op jit(solution)/shard_map/pallas_call | solution.py:420
Async XLA Ops:
  0.6 1.1 %copy-start = (bf16[2048,192]{0,1:T(8,128)(2,1)S(1)}, bf16[2048,192]{0,1:T(8,128)(2,1)}, u32[]{:S(2)}) copy-start(bf16[2048,192]{0,1:T(8,128)(2,1)} %param.8) | copy-start | bytes 2359300
  1.8 1.1 %copy-start.1 = (bf16[2,192,1024]{2,1,0:T(8,128)(2,1)S(1)}, bf16[2,192,1024]{2,1,0:T(8,128)(2,1)}, u32[]{:S(2)}) copy-start(bf16[2,192,1024]{2,1,0:T(8,128)(2,1)} %weights_ref.1) | copy-start | bytes 2359300
  2.9 1.0 %copy-start.2 = (bf16[256,1024]{1,0:T(8,128)(2,1)S(1)}, bf16[256,1024]{1,0:T(8,128)(2,1)}, u32[]{:S(2)}) copy-start(bf16[256,1024]{1,0:T(8,128)(2,1)} %upstream_ref.1) | copy-start | bytes 1572868
  3.9 0.7 %copy-start.3 = (s32[256,5]{0,1:T(8,128)S(1)}, s32[256,5]{0,1:T(8,128)}, u32[]{:S(2)}) copy-start(s32[256,5]{0,1:T(8,128)} %param.12) | copy-start | bytes 15364
  4.6 0.7 %copy-start.4 = (s32[1,8,6]{1,0,2:T(1,128)S(1)}, s32[1,8,6]{1,0,2:T(1,128)}, u32[]{:S(2)}) copy-start(s32[1,8,6]{1,0,2:T(1,128)} %param.10) | copy-start | bytes 580
  5.3 0.7 %copy-start.5 = (s32[256]{0:T(256)S(1)}, s32[256]{0:T(256)}, u32[]{:S(2)}) copy-start(s32[256]{0:T(256)} %param.13) | copy-start | bytes 3076
  6.0 0.7 %copy-start.6 = (s32[256]{0:T(256)S(1)}, s32[256]{0:T(256)}, u32[]{:S(2)}) copy-start(s32[256]{0:T(256)} %param.14) | copy-start | bytes 3076
  6.7 0.7 %copy-start.7 = (s32[1,8]{1,0:T(1,128)S(1)}, s32[1,8]{1,0:T(1,128)}, u32[]{:S(2)}) copy-start(s32[1,8]{1,0:T(1,128)} %counts_ref.1) | copy-start | bytes 100

commit v3 on v2

--- a/solution.py
+++ b/solution.py
@@ -407,14 +407,19 @@
             collective_id=0, has_side_effects=True, vmem_limit_bytes=24 * 1024 * 1024
         ),
     )(
-        request_rows.transpose(2, 0, 1),
-        request_counts,
-        neighbors.T,
-        nbr_counts[None],
-        self_rows[None],
-        feature_table.T,
-        weights,
-        grad_hidden,
+        *(
+            pltpu.with_memory_space_constraint(operand, pltpu.HBM)
+            for operand in (
+                request_rows.transpose(2, 0, 1),
+                request_counts,
+                neighbors.T,
+                nbr_counts[None],
+                self_rows[None],
+                feature_table.T,
+                weights,
+                grad_hidden,
+            )
+        )
     )
     hbm = pl.BlockSpec(memory_space=pltpu.HBM)
     return pl.pallas_call(

time: 45 us -> 38 us (0.84)
  local copies, waits for them, and re-layouts: 6.69 us -> 0 us
    unnamed x16 -> x0, local copies, waits for them, and re-layouts: 6.69 us -> none
where the time goes in v3:
time: 38 us; the launch traced here: 37.8 us
  Pallas kernels  37.2 us (98%)
  between operations  0.64 us (2%)
    pallas_call x1, Pallas kernels, compact_step(): pl.pallas_call(functools.partial(step_kernel, (nodes, feats, caps, fan)),...  35.3 us
    pallas_call x1, Pallas kernels, compact_step(): pl.pallas_call(gradient_kernel, out_shape=(jax.ShapeDtypeStruct((portion,...  1.86 us

profile of v3, /device:TPU:0, one launch (start us, length us, event | category | flops | bytes accessed | tf_op | source)
XLA Modules:
  0.0 37.8 jit_solution(1807172058165175797)
XLA Ops:
  0.6 35.3 %shard_map.95 = (bf16[4,64,256]{2,1,0:T(8,128)(2,1)S(1)}, bf16[4,8,2,48,256]{4,3,2,1,0:T(8,128)(2,1)S(1)}, bf16[192,384]{1,0:T(8,128)(2,1)S(1)}) custom-call(s32[6,1,8]{2,1,0:T(1,128)} %bitcast.7, s32[1,8]{1,0:T(1,128)} %counts_ref.1, s32[5,256]{1,0:T(8,128)} %bitcast.6, s32[1,256]{1,0:T(1,128)} %bitcast.8, s32[1,256]{1,0:T(1,128)} %bitcast.9, ...), custom_call_target="tpu_custom_call" | custom-call | tf_op jit(solution)/shard_map/pallas_call | solution.py:365
  36.0 1.9 %shard_map.96 = (bf16[64,1024]{1,0:T(8,128)(2,1)}, f32[2,192,1024]{2,1,0:T(8,128)}) custom-call(bf16[4,64,256]{2,1,0:T(8,128)(2,1)S(1)} %get-tuple-element.5.hidden_in, bf16[4,8,2,48,256]{4,3,2,1,0:T(8,128)(2,1)S(1)} %get-tuple-element.6.terms, bf16[192,384]{1,0:T(8,128)(2,1)S(1)} %get-tuple-element.7.ordered), custom_call_target="tpu_custom_call" | custom-call | tf_op jit(solution)/shard_map/pallas_call | solution.py:425

commit v4 on v3

--- a/solution.py
+++ b/solution.py
@@ -37,8 +37,8 @@
     upstream,
     ask_out,
     asked,
-    stacked,
-    looked,
+    look_out,
+    look_in,
     front,
     proj,
     preact_ref,
@@ -52,6 +52,8 @@
     look_recv,
     front_send,
     front_recv,
+    order_send,
+    order_recv,
     proj_send,
     proj_recv,
     hid_send,
@@ -117,17 +119,30 @@
         copy = remote(ask_out, asked.at[me], ask_send.at[k], ask_recv.at[me], peer, mine)
         copy.start()
         sends.append(copy)
-    for k, peer in enumerate(feat_peers):
+    flip_y, flip_x, flip_core = 1 - y, 1 - x, 1 - core
+    sibling = 2 * x + flip_core
+    across = (2 * flip_x + core, 2 * flip_x + flip_core)
+    for k, peer in enumerate(across):
         copy = remote(
-            weights_ref.at[:, :, columns(peer)],
-            proj.at[mine],
+            weights_ref.at[y, :, columns(peer)],
+            proj.at[mine, y],
             proj_send.at[k],
-            proj_recv.at[mine],
+            proj_recv.at[mine, y],
             me,
             peer,
         )
         copy.start()
         sends.append(copy)
+    copy = remote(
+        weights_ref.at[:, :, columns(sibling)],
+        proj.at[mine],
+        proj_send.at[2],
+        proj_recv.at[mine, 0],
+        me,
+        sibling,
+    )
+    copy.start()
+    sends.append(copy)
     asked[pl.ds(me, 1)] = ask_out[...][None]
 
     for copy in loads[1:5]:
@@ -164,59 +179,85 @@
 
     for peer in node_peers:
         remote(asked.at[peer], asked.at[peer], ask_send.at[0], ask_recv.at[peer], peer, mine).wait_recv()
-    for r in range(nodes):
-        stacked[r * caps : (r + 1) * caps, :] = asked[r, 0:caps, :]
-    lane = lax.broadcasted_iota(jnp.int32, stacked.shape, 1)
-    wanted = jnp.sum(
-        jnp.where(lane == me, stacked[...].astype(F32), 0.0), axis=1, keepdims=True
-    ).astype(jnp.int32)
+    numbers = asked[...].reshape(nodes * 8, 128).astype(F32)
+    lane = lax.broadcasted_iota(jnp.int32, numbers.shape, 1)
+    wanted = jnp.sum(jnp.where(lane == me, numbers, 0.0), axis=1, keepdims=True)
+    wanted = wanted.astype(jnp.int32)
     rows = table.shape[1]
-    pick = (lax.broadcasted_iota(jnp.int32, (slots, rows), 1) == wanted).astype(F32)
+    pick = (lax.broadcasted_iota(jnp.int32, (nodes * 8, rows), 1) == wanted).astype(F32)
     loads[5].wait()
     found = lax.dot_general(
         pick.astype(BF16), table[...], (((1,), (1,)), ((), ())), preferred_element_type=F32
     )
-    looked[pl.ds(me, 1)] = found.astype(BF16)[None]
+    look_out[...] = found.reshape(look_out.shape)
     for k, peer in enumerate(node_peers):
-        copy = remote(looked.at[me], looked.at[me], look_send.at[k], look_recv.at[me], peer, mine)
+        copy = remote(look_out.at[peer], look_in.at[me], look_send.at[k], look_recv.at[me], peer, mine)
+        copy.start()
+        sends.append(copy)
+    look_in[pl.ds(me, 1)] = look_out[pl.ds(me, 1)]
+
+    def piece(index, layer):
+        return remote(
+            proj.at[index, layer],
+            proj.at[index, layer],
+            proj_send.at[0],
+            proj_recv.at[index, layer],
+            2 * z + flip_y,
+            mine,
+        )
+
+    for k, peer in enumerate(across):
+        piece(peer, y).wait_recv()
+        copy = remote(
+            proj.at[peer, y],
+            proj.at[peer, y],
+            proj_send.at[3 + k],
+            proj_recv.at[peer, y],
+            2 * z + flip_y,
+            mine,
+        )
         copy.start()
         sends.append(copy)
     for peer in node_peers:
-        remote(looked.at[peer], looked.at[peer], look_send.at[0], look_recv.at[peer], peer, mine).wait_recv()
-
-    every = looked[...].reshape(nodes * slots, looked.shape[2])
-
-    def order(requester):
-        row = lax.broadcasted_iota(jnp.int32, (slots, nodes * slots), 0)
-        col = lax.broadcasted_iota(jnp.int32, (slots, nodes * slots), 1)
-        block = owner_of(row)
-        place = block * slots + requester * caps + (row - block * caps)
-        return (col == place).astype(F32).astype(BF16)
-
-    front[pl.ds(mine, 1)] = matmul(order(me), every).astype(BF16)[None]
+        remote(look_in.at[peer], look_in.at[peer], look_send.at[0], look_recv.at[peer], peer, mine).wait_recv()
+
+    row = lax.broadcasted_iota(jnp.int32, (slots, nodes * 8), 0)
+    col = lax.broadcasted_iota(jnp.int32, (slots, nodes * 8), 1)
+    block = owner_of(row)
+    pack = (col == block * 8 + (row - block * caps)).astype(F32).astype(BF16)
+    own_front = matmul(pack, look_in[...].reshape(nodes * 8, look_in.shape[2]).astype(BF16))
+    front[pl.ds(mine, 1)] = own_front.astype(BF16)[None]
+    in_order[pl.ds(me, 1)] = own_front.astype(BF16)[None]
     for k, peer in enumerate(feat_peers):
         copy = remote(front.at[mine], front.at[mine], front_send.at[k], front_recv.at[mine], me, peer)
         copy.start()
         sends.append(copy)
 
-    @pl.loop(0, nodes)
-    def _(r):
-        start = pl.multiple_of(r * slots, slots)
-        in_order[pl.ds(start, slots), :] = matmul(order(r), every).astype(BF16)
-
-    ordered_ref[...] = in_order[...].T
+    for k, peer in enumerate(node_peers):
+        copy = remote(
+            front.at[mine], in_order.at[me], order_send.at[k], order_recv.at[me], peer, mine
+        )
+        copy.start()
+        sends.append(copy)
 
     loads[6].wait()
     preact_ref[...] = jnp.zeros_like(preact_ref)
 
     @pl.loop(0, feats)
     def _(k):
-        index = lax.rem(mine + k, feats)
+        index = 2 * lax.rem(x + k // 2, 2) + lax.rem(core + lax.rem(k, 2), 2)
 
         @pl.when(k > 0)
         def _():
             remote(front.at[index], front.at[index], front_send.at[0], front_recv.at[index], me, index).wait_recv()
-            remote(proj.at[index], proj.at[index], proj_send.at[0], proj_recv.at[index], me, index).wait_recv()
+
+        @pl.when(k == 1)
+        def _():
+            remote(proj.at[index], proj.at[index], proj_send.at[0], proj_recv.at[index, 0], me, index).wait_recv()
+
+        @pl.when(k > 1)
+        def _():
+            piece(index, flip_y).wait_recv()
 
         held = front[pl.ds(index, 1)][0]
         own_rows = matmul(chosen_rows, held).astype(BF16)
@@ -237,7 +278,6 @@
     keep = pltpu.make_async_copy(own_terms, terms.at[mine, me], local_sem.at[8])
     keep.start()
 
-    flip_y, flip_x, flip_core = 1 - y, 1 - x, 1 - core
     depths = [z] + [lax.rem(z + k, depth) for k in range(1, depth)]
     counter = [0]
 
@@ -288,7 +328,11 @@
     keep_rows = pltpu.make_async_copy(out_rows(mine), hidden_ref.at[mine], local_sem.at[9])
     keep_rows.start()
 
-    across = 2 * flip_x + core
+    for peer in node_peers:
+        remote(in_order.at[peer], in_order.at[peer], order_send.at[0], order_recv.at[peer], peer, mine).wait_recv()
+    ordered_ref[...] = in_order[...].reshape(nodes * slots, in_order.shape[2]).T
+
+    across = across[0]
     early = depth // 2
     for k in range(depth):
         node_y, node_x = 2 * depths[k] + flip_y, 2 * depths[k] + y
@@ -381,14 +425,14 @@
             pltpu.VMEM((targets, width), BF16),
             pltpu.VMEM((8, 128), jnp.int32),
             pltpu.VMEM((nodes, 8, 128), jnp.int32),
-            pltpu.VMEM((slots, 128), jnp.int32),
-            pltpu.VMEM((nodes, slots, features), BF16),
+            pltpu.VMEM((nodes, 8, features), F32),
+            pltpu.VMEM((nodes, 8, features), F32),
             pltpu.VMEM((feats, slots, features), BF16),
             pltpu.VMEM((feats, 2, features, width), BF16),
             pltpu.VMEM((targets, width), F32),
             pltpu.VMEM((targets, width), BF16),
             pltpu.VMEM((2, slots, width), BF16),
-            pltpu.VMEM((nodes * slots, features), BF16),
+            pltpu.VMEM((nodes, slots, features), BF16),
             dma((10,)),
             dma((nodes,)),
             dma((nodes,)),
@@ -396,8 +440,10 @@
             dma((nodes,)),
             dma((feats,)),
             dma((feats,)),
-            dma((feats,)),
-            dma((feats,)),
+            dma((nodes,)),
+            dma((nodes,)),
+            dma((5,)),
+            dma((feats, 2)),
             dma((feats,)),
             dma((feats,)),
             dma((moves,)),

time: 38 us -> 37 us (0.974)
  Pallas kernels: 37.2 us -> 36.2 us
    pallas_call x1, Pallas kernels: 35.3 us -> 34.3 us  [compact_step(): pl.pallas_call(functools.partial(step_kernel, (nodes, feats, caps, fan)),...]
where the time goes in v4:
time: 37 us; the launch traced here: 36.8 us
  Pallas kernels  36.2 us (98%)
  between operations  0.64 us (2%)
    pallas_call x1, Pallas kernels, compact_step(): pl.pallas_call(functools.partial(step_kernel, (nodes, feats, caps, fan)),...  34.3 us
    pallas_call x1, Pallas kernels, compact_step(): pl.pallas_call(gradient_kernel, out_shape=(jax.ShapeDtypeStruct((portion,...  1.86 us

profile of v4, /device:TPU:0, one launch (start us, length us, event | category | flops | bytes accessed | tf_op | source)
XLA Modules:
  0.0 36.8 jit_solution(11436805303216963358)
XLA Ops:
  0.6 34.3 %shard_map.95 = (bf16[4,64,256]{2,1,0:T(8,128)(2,1)S(1)}, bf16[4,8,2,48,256]{4,3,2,1,0:T(8,128)(2,1)S(1)}, bf16[192,384]{1,0:T(8,128)(2,1)S(1)}) custom-call(s32[6,1,8]{2,1,0:T(1,128)} %bitcast.7, s32[1,8]{1,0:T(1,128)} %counts_ref.1, s32[5,256]{1,0:T(8,128)} %bitcast.6, s32[1,256]{1,0:T(1,128)} %bitcast.8, s32[1,256]{1,0:T(1,128)} %bitcast.9, ...), custom_call_target="tpu_custom_call" | custom-call | tf_op jit(solution)/shard_map/pallas_call | solution.py:409
  34.9 1.9 %shard_map.96 = (bf16[64,1024]{1,0:T(8,128)(2,1)}, f32[2,192,1024]{2,1,0:T(8,128)}) custom-call(bf16[4,64,256]{2,1,0:T(8,128)(2,1)S(1)} %get-tuple-element.5.hidden_in, bf16[4,8,2,48,256]{4,3,2,1,0:T(8,128)(2,1)S(1)} %get-tuple-element.6.terms, bf16[192,384]{1,0:T(8,128)(2,1)S(1)} %get-tuple-element.7.ordered), custom_call_target="tpu_custom_call" | custom-call | tf_op jit(solution)/shard_map/pallas_call | solution.py:471

commit v5 on v4

--- a/solution.py
+++ b/solution.py
@@ -278,7 +278,13 @@
     keep = pltpu.make_async_copy(own_terms, terms.at[mine, me], local_sem.at[8])
     keep.start()
 
-    depths = [z] + [lax.rem(z + k, depth) for k in range(1, depth)]
+    if depth == 4:
+        half_z, turned = z // 2, z // 2 + z % 2 - 2 * (z // 2) * (z % 2)
+        depths = [z] + [
+            near + half_z * (3 - 2 * near) for near in (1 - turned, 2, 3)
+        ]
+    else:
+        depths = [z] + [lax.rem(z + k, depth) for k in range(1, depth)]
     counter = [0]
 
     def pass_on(node, feat, to_node, to_feat, src=None):
@@ -307,14 +313,13 @@
     to_y = (2 * z + flip_y, mine)
     to_x = (me, 2 * flip_x + core)
     to_core = (me, 2 * x + flip_core)
+    def spread(k):
+        for target in (to_y, to_x, to_core):
+            pass_on(2 * depths[k] + y, mine, *target, src=own_terms if k == 0 else None)
+
     for k in range(1, depth):
         pass_on(me, mine, 2 * depths[k] + y, mine, own_terms)
-    for k in range(depth):
-        node = 2 * depths[k] + y
-        if k > 0:
-            arrived(node, mine)
-        for target in (to_y, to_x, to_core):
-            pass_on(node, mine, *target, src=own_terms if k == 0 else None)
+    spread(0)
 
     hid_out[...] = (preact * half).astype(BF16)
 
@@ -333,17 +338,24 @@
     ordered_ref[...] = in_order[...].reshape(nodes * slots, in_order.shape[2]).T
 
     across = across[0]
-    early = depth // 2
-    for k in range(depth):
+    early = 1
+
+    def turn(k):
         node_y, node_x = 2 * depths[k] + flip_y, 2 * depths[k] + y
         arrived(node_y, mine)
         if k < early:
             pass_on(node_y, mine, *to_x)
+        pass_on(node_y, mine, *to_core)
         arrived(node_x, across)
         if k >= early:
             pass_on(node_x, across, *to_y)
-        pass_on(node_y, mine, *to_core)
         pass_on(node_x, across, *to_core)
+
+    for k in range(1, depth):
+        arrived(2 * depths[k] + y, mine)
+        spread(k)
+        turn(k - 1)
+    turn(depth - 1)
 
     for k in range(depth):
         node = 2 * depths[k] + flip_y

time: 37 us -> 38.7 us (1.046)
  Pallas kernels: 36.2 us -> 37.9 us
    pallas_call x1, Pallas kernels: 34.3 us -> 36 us  [compact_step(): pl.pallas_call(functools.partial(step_kernel, (nodes, feats, caps, fan)),...]
where the time goes in v5:
time: 38.7 us; the launch traced here: 38.5 us
  Pallas kernels  37.9 us (98%)
  between operations  0.64 us (2%)
    pallas_call x1, Pallas kernels, compact_step(): pl.pallas_call(functools.partial(step_kernel, (nodes, feats, caps, fan)),...  36 us
    pallas_call x1, Pallas kernels, compact_step(): pl.pallas_call(gradient_kernel, out_shape=(jax.ShapeDtypeStruct((portion,...  1.87 us

profile of v5, /device:TPU:0, one launch (start us, length us, event | category | flops | bytes accessed | tf_op | source)
XLA Modules:
  0.0 38.5 jit_solution(4198110983927604610)
XLA Ops:
  0.6 36.0 %shard_map.95 = (bf16[4,64,256]{2,1,0:T(8,128)(2,1)S(1)}, bf16[4,8,2,48,256]{4,3,2,1,0:T(8,128)(2,1)S(1)}, bf16[192,384]{1,0:T(8,128)(2,1)S(1)}) custom-call(s32[6,1,8]{2,1,0:T(1,128)} %bitcast.7, s32[1,8]{1,0:T(1,128)} %counts_ref.1, s32[5,256]{1,0:T(8,128)} %bitcast.6, s32[1,256]{1,0:T(1,128)} %bitcast.8, s32[1,256]{1,0:T(1,128)} %bitcast.9, ...), custom_call_target="tpu_custom_call" | custom-call | tf_op jit(solution)/shard_map/pallas_call | solution.py:421
  36.7 1.9 %shard_map.96 = (bf16[64,1024]{1,0:T(8,128)(2,1)}, f32[2,192,1024]{2,1,0:T(8,128)}) custom-call(bf16[4,64,256]{2,1,0:T(8,128)(2,1)S(1)} %get-tuple-element.5.hidden_in, bf16[4,8,2,48,256]{4,3,2,1,0:T(8,128)(2,1)S(1)} %get-tuple-element.6.terms, bf16[192,384]{1,0:T(8,128)(2,1)S(1)} %get-tuple-element.7.ordered), custom_call_target="tpu_custom_call" | custom-call | tf_op jit(solution)/shard_map/pallas_call | solution.py:483

commit v6 on v5

--- a/solution.py
+++ b/solution.py
@@ -206,7 +206,8 @@
             mine,
         )
 
-    for k, peer in enumerate(across):
+    def pass_along(k):
+        peer = across[k]
         piece(peer, y).wait_recv()
         copy = remote(
             proj.at[peer, y],
@@ -218,6 +219,8 @@
         )
         copy.start()
         sends.append(copy)
+
+    pass_along(0)
     for peer in node_peers:
         remote(look_in.at[peer], look_in.at[peer], look_send.at[0], look_recv.at[peer], peer, mine).wait_recv()
 
@@ -240,6 +243,7 @@
         copy.start()
         sends.append(copy)
 
+    pass_along(1)
     loads[6].wait()
     preact_ref[...] = jnp.zeros_like(preact_ref)
 
@@ -285,20 +289,19 @@
         ]
     else:
         depths = [z] + [lax.rem(z + k, depth) for k in range(1, depth)]
-    counter = [0]
+    passed = []
 
     def pass_on(node, feat, to_node, to_feat, src=None):
         copy = remote(
             terms.at[feat, node] if src is None else src,
             terms.at[feat, node],
-            term_send.at[counter[0]],
+            term_send.at[len(passed)],
             term_recv.at[feat, node],
             to_node,
             to_feat,
         )
-        counter[0] += 1
-        copy.start()
-        sends.append(copy)
+        copy.start()
+        passed.append(copy)
 
     def arrived(node, feat):
         remote(
@@ -313,6 +316,7 @@
     to_y = (2 * z + flip_y, mine)
     to_x = (me, 2 * flip_x + core)
     to_core = (me, 2 * x + flip_core)
+
     def spread(k):
         for target in (to_y, to_x, to_core):
             pass_on(2 * depths[k] + y, mine, *target, src=own_terms if k == 0 else None)
@@ -320,6 +324,8 @@
     for k in range(1, depth):
         pass_on(me, mine, 2 * depths[k] + y, mine, own_terms)
     spread(0)
+    arrived(2 * depths[1] + y, mine)
+    spread(1)
 
     hid_out[...] = (preact * half).astype(BF16)
 
@@ -333,12 +339,20 @@
     keep_rows = pltpu.make_async_copy(out_rows(mine), hidden_ref.at[mine], local_sem.at[9])
     keep_rows.start()
 
+    arrived(2 * depths[2] + y, mine)
+    spread(2)
+
     for peer in node_peers:
         remote(in_order.at[peer], in_order.at[peer], order_send.at[0], order_recv.at[peer], peer, mine).wait_recv()
     ordered_ref[...] = in_order[...].reshape(nodes * slots, in_order.shape[2]).T
+    for k in range(3, depth):
+        arrived(2 * depths[k] + y, mine)
+        spread(k)
+    for copy in sends:
+        copy.wait_send()
 
     across = across[0]
-    early = 1
+    early = depth // 2
 
     def turn(k):
         node_y, node_x = 2 * depths[k] + flip_y, 2 * depths[k] + y
@@ -351,11 +365,10 @@
             pass_on(node_x, across, *to_y)
         pass_on(node_x, across, *to_core)
 
-    for k in range(1, depth):
-        arrived(2 * depths[k] + y, mine)
-        spread(k)
-        turn(k - 1)
-    turn(depth - 1)
+    for k in range(depth):
+        turn(k)
+    for copy in passed[: 2 * depth]:
+        copy.wait_send()
 
     for k in range(depth):
         node = 2 * depths[k] + flip_y
@@ -366,7 +379,7 @@
             arrived(node, feat)
     for peer in feat_peers:
         remote(hidden_ref.at[peer], hidden_ref.at[peer], hid_send.at[0], hid_recv.at[peer], me, peer).wait_recv()
-    for copy in sends:
+    for copy in passed[2 * depth :]:
         copy.wait_send()
     keep.wait()
     keep_rows.wait()
@@ -578,7 +591,7 @@
     def per_slice(feature_table, weights, request_rows, *others):
         slots = nodes * request_rows.shape[2]
         plan = per_device
-        if feats == 4 and nodes % 2 == 0 and slots % 16 == 0 and slots <= 128 and request_rows.shape[2] <= 8:
+        if feats == 4 and nodes % 2 == 0 and nodes >= 6 and slots % 16 == 0 and slots <= 128 and request_rows.shape[2] <= 8:
             plan = compact_step
         return plan(feature_table, weights, request_rows, *others)
 

time: 38.7 us -> 37.5 us (0.969)
  Pallas kernels: 37.9 us -> 36.6 us
    pallas_call x1, Pallas kernels: 36 us -> 34.8 us  [compact_step(): pl.pallas_call(functools.partial(step_kernel, (nodes, feats, caps, fan)),...]
where the time goes in v6:
time: 37.5 us; the launch traced here: 37.3 us
  Pallas kernels  36.6 us (98%)
  between operations  0.64 us (2%)
    pallas_call x1, Pallas kernels, compact_step(): pl.pallas_call(functools.partial(step_kernel, (nodes, feats, caps, fan)),...  34.8 us
    pallas_call x1, Pallas kernels, compact_step(): pl.pallas_call(gradient_kernel, out_shape=(jax.ShapeDtypeStruct((portion,...  1.87 us

profile of v6, /device:TPU:0, one launch (start us, length us, event | category | flops | bytes accessed | tf_op | source)
XLA Modules:
  0.0 37.3 jit_solution(7624305151232979481)
XLA Ops:
  0.6 34.8 %shard_map.95 = (bf16[4,64,256]{2,1,0:T(8,128)(2,1)S(1)}, bf16[4,8,2,48,256]{4,3,2,1,0:T(8,128)(2,1)S(1)}, bf16[192,384]{1,0:T(8,128)(2,1)S(1)}) custom-call(s32[6,1,8]{2,1,0:T(1,128)} %bitcast.7, s32[1,8]{1,0:T(1,128)} %counts_ref.1, s32[5,256]{1,0:T(8,128)} %bitcast.6, s32[1,256]{1,0:T(1,128)} %bitcast.8, s32[1,256]{1,0:T(1,128)} %bitcast.9, ...), custom_call_target="tpu_custom_call" | custom-call | tf_op jit(solution)/shard_map/pallas_call | solution.py:434
  35.4 1.9 %shard_map.96 = (bf16[64,1024]{1,0:T(8,128)(2,1)}, f32[2,192,1024]{2,1,0:T(8,128)}) custom-call(bf16[4,64,256]{2,1,0:T(8,128)(2,1)S(1)} %get-tuple-element.5.hidden_in, bf16[4,8,2,48,256]{4,3,2,1,0:T(8,128)(2,1)S(1)} %get-tuple-element.6.terms, bf16[192,384]{1,0:T(8,128)(2,1)S(1)} %get-tuple-element.7.ordered), custom_call_target="tpu_custom_call" | custom-call | tf_op jit(solution)/shard_map/pallas_call | solution.py:496

commit v7 on v6

--- a/solution.py
+++ b/solution.py
@@ -41,7 +41,8 @@
     look_in,
     front,
     proj,
-    preact_ref,
+    part_out,
+    part_in,
     hid_out,
     own_terms,
     in_order,
@@ -56,6 +57,8 @@
     order_recv,
     proj_send,
     proj_recv,
+    part_send,
+    part_recv,
     hid_send,
     hid_recv,
     term_send,
@@ -94,8 +97,9 @@
             (self_ref, self_rows),
             (counts_ref, counts),
             (table_ref, table),
-            (weights_ref.at[:, :, my_columns], proj.at[mine]),
             (upstream_ref.at[:, my_columns], upstream),
+            (weights_ref.at[:, :, columns(core)], proj.at[core, 0]),
+            (weights_ref.at[:, :, columns(2 + core)], proj.at[core, 1]),
         )
     ):
         copy = pltpu.make_async_copy(src, dst, local_sem.at[k])
@@ -121,28 +125,17 @@
         sends.append(copy)
     flip_y, flip_x, flip_core = 1 - y, 1 - x, 1 - core
     sibling = 2 * x + flip_core
-    across = (2 * flip_x + core, 2 * flip_x + flip_core)
-    for k, peer in enumerate(across):
+    for half in range(2):
         copy = remote(
-            weights_ref.at[y, :, columns(peer)],
-            proj.at[mine, y],
-            proj_send.at[k],
-            proj_recv.at[mine, y],
+            weights_ref.at[:, :, columns(2 * half + flip_core)],
+            proj.at[core, half],
+            proj_send.at[half],
+            proj_recv.at[half],
             me,
-            peer,
+            sibling,
         )
         copy.start()
         sends.append(copy)
-    copy = remote(
-        weights_ref.at[:, :, columns(sibling)],
-        proj.at[mine],
-        proj_send.at[2],
-        proj_recv.at[mine, 0],
-        me,
-        sibling,
-    )
-    copy.start()
-    sends.append(copy)
     asked[pl.ds(me, 1)] = ask_out[...][None]
 
     for copy in loads[1:5]:
@@ -196,31 +189,6 @@
         sends.append(copy)
     look_in[pl.ds(me, 1)] = look_out[pl.ds(me, 1)]
 
-    def piece(index, layer):
-        return remote(
-            proj.at[index, layer],
-            proj.at[index, layer],
-            proj_send.at[0],
-            proj_recv.at[index, layer],
-            2 * z + flip_y,
-            mine,
-        )
-
-    def pass_along(k):
-        peer = across[k]
-        piece(peer, y).wait_recv()
-        copy = remote(
-            proj.at[peer, y],
-            proj.at[peer, y],
-            proj_send.at[3 + k],
-            proj_recv.at[peer, y],
-            2 * z + flip_y,
-            mine,
-        )
-        copy.start()
-        sends.append(copy)
-
-    pass_along(0)
     for peer in node_peers:
         remote(look_in.at[peer], look_in.at[peer], look_send.at[0], look_recv.at[peer], peer, mine).wait_recv()
 
@@ -229,57 +197,65 @@
     block = owner_of(row)
     pack = (col == block * 8 + (row - block * caps)).astype(F32).astype(BF16)
     own_front = matmul(pack, look_in[...].reshape(nodes * 8, look_in.shape[2]).astype(BF16))
-    front[pl.ds(mine, 1)] = own_front.astype(BF16)[None]
+    front[pl.ds(core, 1)] = own_front.astype(BF16)[None]
+    copy = remote(
+        front.at[core], front.at[core], front_send.at[0], front_recv.at[0], me, sibling
+    )
+    copy.start()
+    sends.append(copy)
     in_order[pl.ds(me, 1)] = own_front.astype(BF16)[None]
-    for k, peer in enumerate(feat_peers):
-        copy = remote(front.at[mine], front.at[mine], front_send.at[k], front_recv.at[mine], me, peer)
-        copy.start()
-        sends.append(copy)
-
     for k, peer in enumerate(node_peers):
         copy = remote(
-            front.at[mine], in_order.at[me], order_send.at[k], order_recv.at[me], peer, mine
+            front.at[core], in_order.at[me], order_send.at[k], order_recv.at[me], peer, mine
         )
         copy.start()
         sends.append(copy)
 
-    pass_along(1)
-    loads[6].wait()
-    preact_ref[...] = jnp.zeros_like(preact_ref)
-
-    @pl.loop(0, feats)
-    def _(k):
-        index = 2 * lax.rem(x + k // 2, 2) + lax.rem(core + lax.rem(k, 2), 2)
-
-        @pl.when(k > 0)
-        def _():
-            remote(front.at[index], front.at[index], front_send.at[0], front_recv.at[index], me, index).wait_recv()
-
-        @pl.when(k == 1)
-        def _():
-            remote(proj.at[index], proj.at[index], proj_send.at[0], proj_recv.at[index, 0], me, index).wait_recv()
-
-        @pl.when(k > 1)
-        def _():
-            piece(index, flip_y).wait_recv()
-
-        held = front[pl.ds(index, 1)][0]
-        own_rows = matmul(chosen_rows, held).astype(BF16)
-        averaged = (matmul(tally_rows, held) * share_rows).astype(BF16)
-        weight = proj[pl.ds(index, 1)][0]
-        preact_ref[...] += matmul(own_rows, weight[0]) + matmul(averaged, weight[1])
-
-    preact = preact_ref[...]
+    for copy in loads[7:]:
+        copy.wait()
+    for half in range(2):
+        remote(
+            proj.at[flip_core, half], proj.at[flip_core, half], proj_send.at[half], proj_recv.at[half], me, sibling
+        ).wait_recv()
+    remote(
+        front.at[flip_core], front.at[flip_core], front_send.at[0], front_recv.at[0], me, sibling
+    ).wait_recv()
+
+    def for_x(index):
+        weight = [proj[pl.ds(k, 1), pl.ds(index, 1)][0, 0] for k in range(2)]
+        return [
+            matmul(front[0], weight[0][layer]) + matmul(front[1], weight[1][layer])
+            for layer in range(2)
+        ]
+
+    away = for_x(flip_x)
+    part_out[0] = away[0]
+    part_out[1] = away[1]
+    copy = remote(
+        part_out, part_in, part_send.at[0], part_recv.at[0], me, 2 * flip_x + core
+    )
+    copy.start()
+    sends.append(copy)
+    kept = for_x(x)
+    copy.wait_recv()
+
+    def wide(rows_of, values):
+        high = values.astype(BF16)
+        low = (values - high.astype(F32)).astype(BF16)
+        return matmul(rows_of, high) + matmul(rows_of, low)
+
+    preact = wide(chosen_rows, kept[0] + part_in[0])
+    preact = preact + wide(tally_rows, kept[1] + part_in[1]) * share_rows
     square = preact * preact
     bent = jnp.tanh(0.7978845608 * (preact + 0.044715 * preact * square))
     rise = 0.7978845608 * (1.0 + 3.0 * 0.044715 * square)
     half = 0.5 * (1.0 + bent)
-    loads[7].wait()
+    loads[6].wait()
     slope = upstream[...].astype(F32) * (half + 0.5 * preact * (1.0 - bent * bent) * rise)
     both = matmul(back, slope.astype(BF16))
     own_terms[0] = both[:slots].astype(BF16)
     own_terms[1] = (both[slots : 2 * slots] + both[2 * slots :]).astype(BF16)
-    keep = pltpu.make_async_copy(own_terms, terms.at[mine, me], local_sem.at[8])
+    keep = pltpu.make_async_copy(own_terms, terms.at[mine, me], local_sem.at[9])
     keep.start()
 
     if depth == 4:
@@ -336,7 +312,7 @@
         copy = remote(out_rows(peer), hidden_ref.at[mine], hid_send.at[k], hid_recv.at[mine], me, peer)
         copy.start()
         sends.append(copy)
-    keep_rows = pltpu.make_async_copy(out_rows(mine), hidden_ref.at[mine], local_sem.at[9])
+    keep_rows = pltpu.make_async_copy(out_rows(mine), hidden_ref.at[mine], local_sem.at[10])
     keep_rows.start()
 
     arrived(2 * depths[2] + y, mine)
@@ -351,7 +327,7 @@
     for copy in sends:
         copy.wait_send()
 
-    across = across[0]
+    across = 2 * flip_x + core
     early = depth // 2
 
     def turn(k):
@@ -452,23 +428,26 @@
             pltpu.VMEM((nodes, 8, 128), jnp.int32),
             pltpu.VMEM((nodes, 8, features), F32),
             pltpu.VMEM((nodes, 8, features), F32),
-            pltpu.VMEM((feats, slots, features), BF16),
-            pltpu.VMEM((feats, 2, features, width), BF16),
-            pltpu.VMEM((targets, width), F32),
+            pltpu.VMEM((2, slots, features), BF16),
+            pltpu.VMEM((2, 2, 2, features, width), BF16),
+            pltpu.VMEM((2, slots, width), F32),
+            pltpu.VMEM((2, slots, width), F32),
             pltpu.VMEM((targets, width), BF16),
             pltpu.VMEM((2, slots, width), BF16),
             pltpu.VMEM((nodes, slots, features), BF16),
-            dma((10,)),
+            dma((11,)),
             dma((nodes,)),
             dma((nodes,)),
             dma((nodes,)),
             dma((nodes,)),
-            dma((feats,)),
-            dma((feats,)),
+            dma((1,)),
+            dma((1,)),
             dma((nodes,)),
             dma((nodes,)),
-            dma((5,)),
-            dma((feats, 2)),
+            dma((2,)),
+            dma((2,)),
+            dma((1,)),
+            dma((1,)),
             dma((feats,)),
             dma((feats,)),
             dma((moves,)),

time: 37.5 us -> 38.9 us (1.037)
  Pallas kernels: 36.6 us -> 38.1 us
    pallas_call x1, Pallas kernels: 34.8 us -> 36.2 us  [compact_step(): pl.pallas_call(functools.partial(step_kernel, (nodes, feats, caps, fan)),...]
where the time goes in v7:
time: 38.9 us; the launch traced here: 38.7 us
  Pallas kernels  38.1 us (98%)
  between operations  0.64 us (2%)
    pallas_call x1, Pallas kernels, compact_step(): pl.pallas_call(functools.partial(step_kernel, (nodes, feats, caps, fan)),...  36.2 us
    pallas_call x1, Pallas kernels, compact_step(): pl.pallas_call(gradient_kernel, out_shape=(jax.ShapeDtypeStruct((portion,...  1.86 us

profile of v7, /device:TPU:0, one launch (start us, length us, event | category | flops | bytes accessed | tf_op | source)
XLA Modules:
  0.0 38.7 jit_solution(340805082936903617)
XLA Ops:
  0.6 36.2 %shard_map.95 = (bf16[4,64,256]{2,1,0:T(8,128)(2,1)S(1)}, bf16[4,8,2,48,256]{4,3,2,1,0:T(8,128)(2,1)S(1)}, bf16[192,384]{1,0:T(8,128)(2,1)S(1)}) custom-call(s32[6,1,8]{2,1,0:T(1,128)} %bitcast.7, s32[1,8]{1,0:T(1,128)} %counts_ref.1, s32[5,256]{1,0:T(8,128)} %bitcast.6, s32[1,256]{1,0:T(1,128)} %bitcast.8, s32[1,256]{1,0:T(1,128)} %bitcast.9, ...), custom_call_target="tpu_custom_call" | custom-call | tf_op jit(solution)/shard_map/pallas_call | solution.py:410
  36.9 1.9 %shard_map.96 = (bf16[64,1024]{1,0:T(8,128)(2,1)}, f32[2,192,1024]{2,1,0:T(8,128)}) custom-call(bf16[4,64,256]{2,1,0:T(8,128)(2,1)S(1)} %get-tuple-element.5.hidden_in, bf16[4,8,2,48,256]{4,3,2,1,0:T(8,128)(2,1)S(1)} %get-tuple-element.6.terms, bf16[192,384]{1,0:T(8,128)(2,1)S(1)} %get-tuple-element.7.ordered), custom_call_target="tpu_custom_call" | custom-call | tf_op jit(solution)/shard_map/pallas_call | solution.py:475

commit v8 on v6

--- a/solution.py
+++ b/solution.py
@@ -108,11 +108,13 @@
     for peer in feat_peers:
         pl.semaphore_signal(barrier, inc=1, device_id=(me, peer), device_id_type=MESH)
 
+    corner = (2 * z + 1 - y, 2 * (1 - x) + core)
+    pl.semaphore_signal(barrier, inc=1, device_id=corner, device_id_type=MESH)
     ask_out[...] = jnp.zeros_like(ask_out)
     loads[0].wait()
     for k in range(caps):
         ask_out[k : k + 1, 0:nodes] = request[k]
-    pl.semaphore_wait(barrier, nodes + feats - 2)
+    pl.semaphore_wait(barrier, nodes + feats - 1)
 
     sends = []
     for k, peer in enumerate(node_peers):
@@ -221,6 +223,7 @@
         sends.append(copy)
 
     pass_along(0)
+    pass_along(1)
     for peer in node_peers:
         remote(look_in.at[peer], look_in.at[peer], look_send.at[0], look_recv.at[peer], peer, mine).wait_recv()
 
@@ -243,7 +246,6 @@
         copy.start()
         sends.append(copy)
 
-    pass_along(1)
     loads[6].wait()
     preact_ref[...] = jnp.zeros_like(preact_ref)
 
@@ -320,6 +322,8 @@
     def spread(k):
         for target in (to_y, to_x, to_core):
             pass_on(2 * depths[k] + y, mine, *target, src=own_terms if k == 0 else None)
+        if k >= 2:
+            pass_on(2 * depths[k] + y, mine, *corner)
 
     for k in range(1, depth):
         pass_on(me, mine, 2 * depths[k] + y, mine, own_terms)
@@ -352,16 +356,15 @@
         copy.wait_send()
 
     across = across[0]
-    early = depth // 2
 
     def turn(k):
         node_y, node_x = 2 * depths[k] + flip_y, 2 * depths[k] + y
         arrived(node_y, mine)
-        if k < early:
+        if k == 0:
             pass_on(node_y, mine, *to_x)
         pass_on(node_y, mine, *to_core)
         arrived(node_x, across)
-        if k >= early:
+        if k == 1:
             pass_on(node_x, across, *to_y)
         pass_on(node_x, across, *to_core)
 

time: 37.5 us -> 36.4 us (0.971)
  Pallas kernels: 36.6 us -> 35.5 us
    pallas_call x1, Pallas kernels: 34.8 us -> 33.7 us  [compact_step(): pl.pallas_call(functools.partial(step_kernel, (nodes, feats, caps, fan)),...]
where the time goes in v8:
time: 36.4 us; the launch traced here: 36.2 us
  Pallas kernels  35.5 us (98%)
  between operations  0.64 us (2%)
    pallas_call x1, Pallas kernels, compact_step(): pl.pallas_call(functools.partial(step_kernel, (nodes, feats, caps, fan)),...  33.7 us
    pallas_call x1, Pallas kernels, compact_step(): pl.pallas_call(gradient_kernel, out_shape=(jax.ShapeDtypeStruct((portion,...  1.86 us

profile of v8, /device:TPU:0, one launch (start us, length us, event | category | flops | bytes accessed | tf_op | source)
XLA Modules:
  0.0 36.2 jit_solution(2651571511502503176)
XLA Ops:
  0.6 33.7 %shard_map.95 = (bf16[4,64,256]{2,1,0:T(8,128)(2,1)S(1)}, bf16[4,8,2,48,256]{4,3,2,1,0:T(8,128)(2,1)S(1)}, bf16[192,384]{1,0:T(8,128)(2,1)S(1)}) custom-call(s32[6,1,8]{2,1,0:T(1,128)} %bitcast.7, s32[1,8]{1,0:T(1,128)} %counts_ref.1, s32[5,256]{1,0:T(8,128)} %bitcast.6, s32[1,256]{1,0:T(1,128)} %bitcast.8, s32[1,256]{1,0:T(1,128)} %bitcast.9, ...), custom_call_target="tpu_custom_call" | custom-call | tf_op jit(solution)/shard_map/pallas_call | solution.py:437
  34.3 1.9 %shard_map.96 = (bf16[64,1024]{1,0:T(8,128)(2,1)}, f32[2,192,1024]{2,1,0:T(8,128)}) custom-call(bf16[4,64,256]{2,1,0:T(8,128)(2,1)S(1)} %get-tuple-element.5.hidden_in, bf16[4,8,2,48,256]{4,3,2,1,0:T(8,128)(2,1)S(1)} %get-tuple-element.6.terms, bf16[192,384]{1,0:T(8,128)(2,1)S(1)} %get-tuple-element.7.ordered), custom_call_target="tpu_custom_call" | custom-call | tf_op jit(solution)/shard_map/pallas_call | solution.py:499

commit v9 on v8

--- a/solution.py
+++ b/solution.py
@@ -322,7 +322,7 @@
     def spread(k):
         for target in (to_y, to_x, to_core):
             pass_on(2 * depths[k] + y, mine, *target, src=own_terms if k == 0 else None)
-        if k >= 2:
+        if k >= 1:
             pass_on(2 * depths[k] + y, mine, *corner)
 
     for k in range(1, depth):
@@ -364,8 +364,6 @@
             pass_on(node_y, mine, *to_x)
         pass_on(node_y, mine, *to_core)
         arrived(node_x, across)
-        if k == 1:
-            pass_on(node_x, across, *to_y)
         pass_on(node_x, across, *to_core)
 
     for k in range(depth):

time: 36.4 us -> 36.6 us (level)
  no operation moved by 1% of the time
where the time goes in v9:
time: 36.6 us; the launch traced here: 36.4 us
  Pallas kernels  35.8 us (98%)
  between operations  0.64 us (2%)
    pallas_call x1, Pallas kernels, compact_step(): pl.pallas_call(functools.partial(step_kernel, (nodes, feats, caps, fan)),...  33.9 us
    pallas_call x1, Pallas kernels, compact_step(): pl.pallas_call(gradient_kernel, out_shape=(jax.ShapeDtypeStruct((portion,...  1.87 us

profile of v9, /device:TPU:0, one launch (start us, length us, event | category | flops | bytes accessed | tf_op | source)
XLA Modules:
  0.0 36.4 jit_solution(11864821450535789324)
XLA Ops:
  0.6 33.9 %shard_map.95 = (bf16[4,64,256]{2,1,0:T(8,128)(2,1)S(1)}, bf16[4,8,2,48,256]{4,3,2,1,0:T(8,128)(2,1)S(1)}, bf16[192,384]{1,0:T(8,128)(2,1)S(1)}) custom-call(s32[6,1,8]{2,1,0:T(1,128)} %bitcast.7, s32[1,8]{1,0:T(1,128)} %counts_ref.1, s32[5,256]{1,0:T(8,128)} %bitcast.6, s32[1,256]{1,0:T(1,128)} %bitcast.8, s32[1,256]{1,0:T(1,128)} %bitcast.9, ...), custom_call_target="tpu_custom_call" | custom-call | tf_op jit(solution)/shard_map/pallas_call | solution.py:435
  34.6 1.9 %shard_map.96 = (bf16[64,1024]{1,0:T(8,128)(2,1)}, f32[2,192,1024]{2,1,0:T(8,128)}) custom-call(bf16[4,64,256]{2,1,0:T(8,128)(2,1)S(1)} %get-tuple-element.5.hidden_in, bf16[4,8,2,48,256]{4,3,2,1,0:T(8,128)(2,1)S(1)} %get-tuple-element.6.terms, bf16[192,384]{1,0:T(8,128)(2,1)S(1)} %get-tuple-element.7.ordered), custom_call_target="tpu_custom_call" | custom-call | tf_op jit(solution)/shard_map/pallas_call | solution.py:497
